TPU v7x, 128 devices: a whole 4x4x4 slice. The times are simulated.
128 devices in a mesh: gx: 8 (over x, core), gy: 16 (over y, z).
Axes of the slice: x: 4, y: 4, z: 4, core: 2. Of those that a mesh axis runs over, the one named last changes fastest.
Arguments:
- atm_blocks: bfloat16 [16384, 30, 256], P(('gx', 'gy')), may hold values from -6 to 6
- tile_dev: int32 [32768, 1], replicated, may hold values from 0 to 127; in each aligned block of 256 rows (0 to 255, 256 to 511, ...) at most 3 rows name the same one
- tile_blk: int32 [32768], replicated, may hold values from 0 to 127
- tile_weights: bfloat16 [32768, 256, 128], P(('gx', 'gy')), may hold values from -0.375 to 0.375
- tile_dst: int32 [32768], P(('gx', 'gy')), may hold values from 0 to 63
- ocean_frac: float32 [8192, 128], P(('gx', 'gy')), may hold values from 0.5 to 1
- halo_send: int32 [128, 2, 8], P(('gx', 'gy')), may hold values from 0 to 63
Outputs:
- ocean_fields: bfloat16 [8192, 30, 128], P(('gx', 'gy'))
- ocean_halo: bfloat16 [128, 2, 8, 30, 128], P(('gx', 'gy'))
Inputs may be any that keep to these rules, and one draw needn't show every extreme that they name: `tile_dev`: within the 256 rows of one device (aligned blocks of rows), no source device is named more than 3 times, and some source device is named exactly 3 times.
All inputs are finite; a program needn't handle non-finite values.
Results may differ from a plain program's by a relative error of at most 0.001.
Values may be sent and summed in bfloat16 or wider, within the bound.
A program may use at most 128 MiB of HBM per device.

v0:
```python
import jax
import jax.numpy as jnp
from jax import lax
from jax.sharding import PartitionSpec as P


def padded_2(cells, sides, width):
    for axis, dim in sides:
        count = lax.axis_size(axis)
        head = lax.slice_in_dim(cells, 0, width, axis=dim)
        tail = lax.slice_in_dim(cells, cells.shape[dim] - width, cells.shape[dim], axis=dim)
        cells = jnp.concatenate(
            [
                lax.ppermute(tail, axis, [(i, (i + 1) % count) for i in range(count)]),
                cells,
                lax.ppermute(head, axis, [((i + 1) % count, i) for i in range(count)]),
            ],
            axis=dim,
        )
    return cells


def per_device(atm_blocks, tile_dev, tile_blk, tile_weights, tile_dst, ocean_frac, halo_send):
    devices = lax.axis_size(("gx", "gy"))
    myself = lax.axis_index(("gx", "gy"))
    per_dev = tile_weights.shape[0]
    capacity = max(2, 3 * per_dev // (2 * devices))
    fields_n = atm_blocks.shape[1]
    nodes = atm_blocks.shape[2]
    cells = tile_weights.shape[2]
    ocean_n = ocean_frac.shape[0]
    blocks_n = atm_blocks.shape[0]
    source_dev = tile_dev[:, 0].reshape(devices, per_dev)
    block_of = tile_blk.reshape(devices, per_dev)
    same_src = source_dev[:, :, None] == source_dev[:, None, :]
    counter = jnp.arange(per_dev, dtype=jnp.int32)
    before = counter[None, :] < counter[:, None]
    position = jnp.sum((same_src & before[None, :, :]).astype(jnp.int32), axis=2)
    mine = source_dev == myself
    slot_ids = jnp.arange(capacity, dtype=jnp.int32)
    matched = mine[:, None, :] & (position[:, None, :] == slot_ids[None, :, None])
    send_index = jnp.sum(jnp.where(matched, block_of[:, None, :], 0), axis=2).reshape(-1)
    slot_used = jnp.any(matched, axis=2).reshape(-1)
    block_ids = jnp.arange(blocks_n, dtype=jnp.int32)
    send_select = ((send_index[:, None] == block_ids[None, :]) & slot_used[:, None]).astype(
        jnp.bfloat16
    )
    outgoing = jnp.dot(
        send_select,
        atm_blocks.reshape(blocks_n, fields_n * nodes),
        preferred_element_type=jnp.float32,
    )
    outgoing = outgoing.astype(jnp.bfloat16).reshape(devices, capacity, fields_n, nodes)
    incoming = lax.all_to_all(outgoing, ("gx", "gy"), split_axis=0, concat_axis=0, tiled=True)
    incoming = incoming.reshape(devices * capacity, fields_n * nodes)
    my_source = lax.dynamic_index_in_dim(source_dev, myself, 0, keepdims=False)
    my_position = lax.dynamic_index_in_dim(position, myself, 0, keepdims=False)
    read_slot = my_source * capacity + my_position
    slot_range = jnp.arange(devices * capacity, dtype=jnp.int32)
    read_select = (read_slot[:, None] == slot_range[None, :]).astype(jnp.bfloat16)
    gathered = jnp.dot(read_select, incoming, preferred_element_type=jnp.float32)
    gathered = gathered.astype(jnp.bfloat16).reshape(per_dev, fields_n, nodes)
    results = jnp.einsum("tfk,tkc->tfc", gathered, tile_weights, preferred_element_type=jnp.float32)
    onehot = (tile_dst[None, :] == jnp.arange(ocean_n, dtype=jnp.int32)[:, None]).astype(
        jnp.float32
    )
    totals = jnp.dot(
        onehot, results.reshape(per_dev, fields_n * cells), precision=lax.Precision.HIGHEST
    )
    ocean_fields = (totals.reshape(ocean_n, fields_n, cells) / ocean_frac[:, None, :]).astype(
        jnp.bfloat16
    )
    rim_list = halo_send[0].reshape(-1)
    rim_count = rim_list.shape[0]
    rim_select = (rim_list[:, None] == jnp.arange(ocean_n, dtype=jnp.int32)[None, :]).astype(
        jnp.bfloat16
    )
    rim_blocks = jnp.dot(
        rim_select,
        ocean_fields.reshape(ocean_n, fields_n * cells),
        preferred_element_type=jnp.float32,
    )
    rim_blocks = rim_blocks.astype(jnp.bfloat16).reshape(2, rim_count // 2, fields_n, cells)
    padded = padded_2(rim_blocks, ((("gx", "gy"), 0),), 1)
    ocean_halo = jnp.stack([padded[0], padded[3]], axis=0)[None]
    return (ocean_fields, ocean_halo)


def solution(mesh):
    in_specs = (
        P(("gx", "gy"), None, None),
        P(),
        P(),
        P(("gx", "gy"), None, None),
        P(("gx", "gy")),
        P(("gx", "gy"), None),
        P(("gx", "gy"), None, None),
    )
    out_specs = (P(("gx", "gy"), None, None), P(("gx", "gy"), None, None, None, None))
    return jax.shard_map(
        per_device, mesh=mesh, in_specs=in_specs, out_specs=out_specs, check_vma=False
    )
```

profile of v0, /device:TPU:0, one launch (start us, length us, event | category | flops | bytes accessed | tf_op | source)
XLA Modules:
  0.0 185.0 jit_solution(1192213636082810630)
XLA Ops:
  0.7 0.5 broadcast.21
  1.2 1.9 %reduce.3 = s32[32768]{0:T(1024)S(1)} reduce(s32[32768,1]{0,1:T(1,128)} %param.8, s32[]{:T(128)} %broadcast.21), dimensions={1}, to_apply=%param.8.reduce_sub_computation.3 | reduce | bytes 262148 | tf_op args[1]
  3.1 10.5 %convert_reduce_fusion = s32[128,256]{1,0:T(8,128)S(1)} fusion(s32[128,256]{1,0:T(8,128)S(1)} %reshape_squeeze.3, pred[256,256]{1,0:T(8,128)(4,1)S(1)} %iota_compare_fusion.3), kind=kLoop, calls=%fused_computation | loop fusion | flops 33521664 | bytes 327680 | tf_op jit(solution)/shard_map/reduce_sum | solution.py:38
  13.6 0.1 fusion.11
  13.8 0.1 copy.16
  13.9 0.2 and.32
  14.1 0.9 broadcast_in_dim.16
  15.1 0.2 select_reduce_fusion
  15.3 0.1 copy.15
  15.4 0.2 eq.106
  15.6 2.8 %copy.17 = bf16[128,30,256]{0,2,1:T(8,128)(2,1)S(1)} copy(bf16[128,30,256]{2,0,1:T(8,128)(2,1)} %param.7) | data formatting | bytes 3932160 | tf_op args[0]
  18.4 4.3 %convolution_convert_fusion = bf16[384,7680]{1,0:T(8,128)(2,1)} fusion(bf16[128,7680]{0,1:T(8,128)(2,1)S(1)} %bitcast.40, s32[384]{0:T(512)S(1)} %eq.106, pred[384]{0:T(512)(128)(4,1)S(1)} %and.32), kind=kOutput, calls=%fused_computation.1 | convolution fusion | flops 758022144 | bytes 7866240 | tf_op jit(solution)/shard_map/dot_general | solution.py:48
  22.7 9.6 %reshape.67 = bf16[128,3,30,256]{3,2,1,0:T(8,128)(2,1)} reshape(bf16[384,7680]{1,0:T(8,128)(2,1)} %convolution_convert_fusion) | data formatting | bytes 11796480 | tf_op jit(solution)/shard_map/reshape | solution.py:53
  32.3 0.0 copy-start.3
  32.3 11.8 %all-to-all-start = ((bf16[128,3,30,256]{3,2,1,0:T(8,128)(2,1)}), bf16[128,3,30,256]{3,2,1,0:T(8,128)(2,1)}, u32[]{:S(2)}, u32[]{:S(2)}) async-start(bf16[128,3,30,256]{3,2,1,0:T(8,128)(2,1)} %reshape.67), calls=%async_computation | async-start | bytes 12582912 | tf_op jit(solution)/shard_map/all_to_all | solution.py:54
  44.1 0.0 copy-done.3
  44.1 0.1 eq.110
  44.2 82.0 %all-to-all-done = bf16[128,3,30,256]{3,2,1,0:T(8,128)(2,1)} async-done(((bf16[128,3,30,256]{3,2,1,0:T(8,128)(2,1)}), bf16[128,3,30,256]{3,2,1,0:T(8,128)(2,1)}, u32[]{:S(2)}, u32[]{:S(2)}) %all-to-all-start) | async-done | bytes 5898272 | tf_op jit(solution)/shard_map/all_to_all | solution.py:54
  126.2 9.7 %copy.23 = bf16[48,8,30,256]{3,1,2,0:T(8,128)(2,1)S(1)} copy(bf16[48,8,30,256]{3,2,1,0:T(8,128)(2,1)} %bitcast.15) | data formatting | bytes 11796480
  135.9 4.1 %convolution_convert_fusion.1 = bf16[256,7680]{1,0:T(8,128)(2,1)} fusion(bf16[384,7680]{1,0:T(8,128)(2,1)S(1)} %bitcast.38, s32[256]{0:T(256)S(1)} %bitcast.41), kind=kOutput, calls=%fused_computation.2 | convolution fusion | flops 1512013824 | bytes 9831424 | tf_op jit(solution)/shard_map/dot_general | solution.py:61
  140.0 6.3 %copy.18 = bf16[256,7680]{0,1:T(8,128)(2,1)} copy(bf16[256,7680]{1,0:T(8,128)(2,1)} %convolution_convert_fusion.1) | data formatting | bytes 7864320 | tf_op jit(solution)/shard_map/convert_element_type | solution.py:62
  146.2 7.9 %copy.19 = bf16[256,30,256]{2,1,0:T(8,128)(2,1)} copy(bf16[256,30,256]{0,2,1:T(8,128)(2,1)} %bitcast.39) | data formatting | bytes 7864320 | tf_op jit(solution)/shard_map/reshape | solution.py:62
  154.1 11.3 %fusion.21 = f32[256,30,128]{2,1,0:T(8,128)} fusion(bf16[256,30,256]{2,1,0:T(8,128)(2,1)} %copy.19, bf16[256,256,128]{2,1,0:T(8,128)(2,1)} %param.10), kind=kOutput, calls=%fused_computation.31 | convolution fusion | flops 503316480 | bytes 24641536 | tf_op jit(solution)/shard_map/tfk,tkc->tfc/dot_general | solution.py:63
  165.4 0.0 copy-start.1
  165.4 0.0 copy-start.2
  165.4 5.2 %copy.20 = f32[256,30,128]{0,2,1:T(8,128)} copy(f32[256,30,128]{2,1,0:T(8,128)} %fusion.21) | data formatting | bytes 7864320 | tf_op jit(solution)/shard_map/tfk,tkc->tfc/dot_general | solution.py:63
  170.6 0.0 copy-done.1
  170.6 0.0 copy-done.2
  170.6 4.2 %fusion.5 = bf16[64,30,128]{2,0,1:T(8,128)(2,1)S(1)} fusion(f32[256,30,128]{0,2,1:T(8,128)} %copy.20, f32[64,128]{1,0:T(8,128)S(1)} %copy-done.1, s32[256]{0:T(256)S(1)} %copy-done.2), kind=kOutput, calls=%fused_computation.7 | convolution fusion | flops 755482624 | bytes 4457472 | tf_op jit(solution)/shard_map/dot_general | solution.py:67
  174.9 0.0 copy-start
  174.9 0.2 convolution_convert_fusion.2
  175.1 0.1 collective-permute-start
  175.2 7.2 %collective-permute-start.1 = (bf16[1,8,30,128]{3,1,2,0:T(8,128)(2,1)S(1)}, bf16[1,8,30,128]{3,1,2,0:T(8,128)(2,1)S(1)}, u32[]{:S(2)}, u32[]{:S(2)}) collective-permute-start(bf16[1,8,30,128]{3,1,2,0:T(8,128)(2,1)S(1)} %get-tuple-element.3), channel_id=1, source_target_pairs={{1,0},{2,1},{3,2},{4,3},{5,4},{6,5},{7,6},{8,7},{9,8},{10,9},{11,1... | collective-permute-start | bytes 184328 | tf_op jit(solution)/shard_map/ppermute | solution.py:16
  182.4 1.9 %collective-permute-done = bf16[1,8,30,128]{3,1,2,0:T(8,128)(2,1)S(1)} collective-permute-done((bf16[1,8,30,128]{3,1,2,0:T(8,128)(2,1)S(1)}, bf16[1,8,30,128]{3,1,2,0:T(8,128)(2,1)S(1)}, u32[]{:S(2)}, u32[]{:S(2)}) %collective-permute-start) | collective-permute-done | bytes 61472 | tf_op jit(solution)/shard_map/ppermute | solution.py:14
  184.3 0.0 collective-permute-done.1
  184.3 0.7 maximum_bitcast_fusion
  185.0 0.0 copy-done
  (5 shorter events, 0.1 us)
Async XLA Ops:
  32.3 11.8 %copy-start.3 = (s32[1,2,8]{2,1,0:T(2,128)S(1)}, s32[1,2,8]{2,1,0:T(2,128)}, u32[]{:S(2)}) copy-start(s32[1,2,8]{2,1,0:T(2,128)} %param.13) | copy-start | bytes 196
  32.3 93.9 %all-to-all-start = ((bf16[128,3,30,256]{3,2,1,0:T(8,128)(2,1)}), bf16[128,3,30,256]{3,2,1,0:T(8,128)(2,1)}, u32[]{:S(2)}, u32[]{:S(2)}) async-start(bf16[128,3,30,256]{3,2,1,0:T(8,128)(2,1)} %reshape.67), calls=%async_computation | async-start | bytes 12582912 | tf_op jit(solution)/shard_map/all_to_all | solution.py:54
  165.4 5.2 %copy-start.1 = (f32[64,128]{1,0:T(8,128)S(1)}, f32[64,128]{1,0:T(8,128)}, u32[]{:S(2)}) copy-start(f32[64,128]{1,0:T(8,128)} %param.12) | copy-start | bytes 98308
  165.4 5.2 %copy-start.2 = (s32[256]{0:T(256)S(1)}, s32[256]{0:T(256)}, u32[]{:S(2)}) copy-start(s32[256]{0:T(256)} %param.11) | copy-start | bytes 3076
  174.9 10.1 %copy-start = (bf16[64,30,128]{2,0,1:T(8,128)(2,1)}, bf16[64,30,128]{2,0,1:T(8,128)(2,1)S(1)}, u32[]{:S(2)}) copy-start(bf16[64,30,128]{2,0,1:T(8,128)(2,1)S(1)} %fusion.5) | copy-start | bytes 1474564
  175.1 9.2 %collective-permute-start = (bf16[1,8,30,128]{3,1,2,0:T(8,128)(2,1)S(1)}, bf16[1,8,30,128]{3,1,2,0:T(8,128)(2,1)S(1)}, u32[]{:S(2)}, u32[]{:S(2)}) collective-permute-start(bf16[1,8,30,128]{3,1,2,0:T(8,128)(2,1)S(1)} %get-tuple-element.2), channel_id=1, source_target_pairs={{0,1},{1,2},{2,3},{3,4},{4,5},{5,6},{6,7},{7,8},{8,9},{9,10},{10,1... | collective-permute-start | bytes 184328 | tf_op jit(solution)/shard_map/ppermute | solution.py:14
  175.2 9.1 %collective-permute-start.1 = (bf16[1,8,30,128]{3,1,2,0:T(8,128)(2,1)S(1)}, bf16[1,8,30,128]{3,1,2,0:T(8,128)(2,1)S(1)}, u32[]{:S(2)}, u32[]{:S(2)}) collective-permute-start(bf16[1,8,30,128]{3,1,2,0:T(8,128)(2,1)S(1)} %get-tuple-element.3), channel_id=1, source_target_pairs={{1,0},{2,1},{3,2},{4,3},{5,4},{6,5},{7,6},{8,7},{9,8},{10,9},{11,1... | collective-permute-start | bytes 184328 | tf_op jit(solution)/shard_map/ppermute | solution.py:16
where the time goes:
time: 186 us; the launch traced here: 185 us
  waiting for transfers between devices  83.9 us (45%)
  local copies, waits for them, and re-layouts  43.7 us (23%)
  matrix products  24.2 us (13%)
  starting transfers between devices  19 us (10%)
  other arithmetic  13.4 us (7%)
    all_to_all x1, waiting for transfers between devices, per_device(): lax.all_to_all(outgoing, ('gx', 'gy'), split_axis=0, concat_axis=0, tiled...  82 us
    unnamed x11, local copies, waits for them, and re-layouts  13.1 us
    all_to_all x1, starting transfers between devices, per_device(): lax.all_to_all(outgoing, ('gx', 'gy'), split_axis=0, concat_axis=0, tiled...  11.8 us
    dot_general x1, matrix products, per_device(): jnp.einsum('tfk,tkc->tfc', gathered, tile_weights, preferred_element_type...  11.3 us
    reduce_sum x1, other arithmetic, per_device(): jnp.sum((same_src & before[None, :, :]).astype(jnp.int32), axis=2)  10.5 us
    reshape x1, local copies, waits for them, and re-layouts, per_device(): outgoing.astype(jnp.bfloat16).reshape(devices, capacity, fields_n, nodes)  9.55 us
    reshape x1, local copies, waits for them, and re-layouts, per_device(): gathered = gathered.astype(jnp.bfloat16).reshape(per_dev, fields_n, nodes)  7.85 us
    ppermute x1, starting transfers between devices, padded_2(): lax.ppermute(head, axis, [((i + 1) % count, i) for i in range(count)])  7.16 us
  transfers between devices with their start and end apart: 3, of which 2 were waited for; matrix products, arithmetic and copies ran while one was open for 0% of the time, Pallas kernels for 0%

commit v1 on v0

v1 whole, which is shorter than its diff:
```python
import functools

import jax
import jax.numpy as jnp
from jax import lax
from jax.experimental import pallas as pl
from jax.experimental.pallas import tpu as pltpu
from jax.sharding import PartitionSpec as P

MESH = pl.DeviceIdType.MESH
DEVICES = 128
CAP = 3
GROUP = 21
GROUPS = 6


def step_offset(i):
    j = jnp.where(i < 126, lax.rem(i * 37, 126) + 2, 1)
    return j // 32, lax.rem(j // 8, 4), lax.rem(j // 2, 4), lax.rem(j, 2)


def exchange_kernel(
    send_blk, tile_of, seg_slot, seg_keep, seg_last, halo_idx,
    atm, weights, frac, out_hbm, halo_hbm,
    outgoing, incoming, near, w_vmem, results, running, fields, rim,
    send_sem, recv_sem, near_sem, w_sem, rim_send, rim_recv, out_sem,
):
    gx, gy = lax.axis_index("gx"), lax.axis_index("gy")
    myself = gx * 16 + gy
    x, c, y, z = gx // 2, lax.rem(gx, 2), gy // 4, lax.rem(gy, 4)

    def target(i):
        dx, dy, dz, dc = step_offset(i)
        return lax.rem(x + dx, 4) * 2 + lax.rem(c + dc, 2), lax.rem(y + dy, 4) * 4 + lax.rem(z + dz, 4)

    def source(i):
        dx, dy, dz, dc = step_offset(i)
        gx_s = lax.rem(x - dx + 4, 4) * 2 + lax.rem(c + dc, 2)
        return gx_s * 16 + lax.rem(y - dy + 4, 4) * 4 + lax.rem(z - dz + 4, 4)

    barrier = pltpu.get_barrier_semaphore()

    @pl.loop(0, DEVICES - 1)
    def _(i):
        pl.semaphore_signal(barrier, inc=1, device_id=target(i), device_id_type=MESH)

    w_copy = pltpu.make_async_copy(weights, w_vmem, w_sem)
    w_copy.start()

    def pack(buffer, slot, d):
        for k in range(CAP):
            buffer[slot * CAP + k] = atm[send_blk[d * CAP + k]]

    pack(near, 1, myself)
    pl.semaphore_wait(barrier, DEVICES - 1)

    for g in range(GROUPS):

        @pl.loop(0, GROUP)
        def _(j, g=g):
            i = g * GROUP + j
            dgx, dgy = target(i)
            pack(outgoing, i, dgx * 16 + dgy)
            pltpu.make_async_remote_copy(
                src_ref=outgoing.at[pl.ds(i * CAP, CAP)],
                dst_ref=incoming[g].at[pl.ds(j * CAP, CAP)],
                send_sem=send_sem,
                recv_sem=recv_sem.at[g],
                device_id=(dgx, dgy),
                device_id_type=MESH,
            ).start()

    last = DEVICES - 2
    dgx, dgy = target(last)
    pack(outgoing, last, dgx * 16 + dgy)
    near_copy = pltpu.make_async_remote_copy(
        src_ref=outgoing.at[pl.ds(last * CAP, CAP)],
        dst_ref=near.at[pl.ds(0, CAP)],
        send_sem=near_sem.at[0],
        recv_sem=near_sem.at[1],
        device_id=(dgx, dgy),
        device_id_type=MESH,
    )
    near_copy.start()
    w_copy.wait()

    def multiply(buffer, slot, s):
        for k in range(CAP):
            results[s * CAP + k] = jnp.dot(
                buffer[slot * CAP + k], w_vmem[tile_of[s * CAP + k]], preferred_element_type=jnp.float32
            )

    multiply(near, 1, myself)
    near_copy.wait()
    multiply(near, 0, source(last))
    for g in range(GROUPS):
        pltpu.make_async_copy(incoming[g], incoming[g], recv_sem.at[g]).wait()

        @pl.loop(0, GROUP)
        def _(j, g=g):
            multiply(incoming[g], j, source(g * GROUP + j))

    tiles = running.shape[0]

    def add(r, total):
        total = total * seg_keep[r].astype(jnp.float32) + results[seg_slot[r]]
        running[r] = total
        return total

    lax.fori_loop(0, tiles, add, jnp.zeros(running.shape[1:], jnp.float32))

    @pl.loop(0, fields.shape[0])
    def _(b):
        end = seg_last[b]
        total = jnp.where(end >= 0, running[jnp.maximum(end, 0)], 0.0)
        fields[b] = (total / frac[pl.ds(b, 1), :]).astype(jnp.bfloat16)

    out_copy = pltpu.make_async_copy(fields, out_hbm, out_sem)
    out_copy.start()
    rim_n = rim.shape[0] // 2
    for j in range(2 * rim_n):
        rim[j] = fields[halo_idx[j]]
    up, down = lax.rem(myself + 1, DEVICES), lax.rem(myself + DEVICES - 1, DEVICES)
    rim_copies = []
    for side, there in ((1, up), (0, down)):
        copy = pltpu.make_async_remote_copy(
            src_ref=rim.at[pl.ds(side * rim_n, rim_n)],
            dst_ref=halo_hbm.at[1 - side],
            send_sem=rim_send.at[side],
            recv_sem=rim_recv.at[side],
            device_id=(there // 16, lax.rem(there, 16)),
            device_id_type=MESH,
        )
        copy.start()
        rim_copies.append(copy)
    for copy in rim_copies:
        copy.wait()
    out_copy.wait()
    body = outgoing.at[pl.ds(0, (DEVICES - 2) * CAP)]
    pltpu.make_async_copy(body, body, send_sem).wait()


def per_device(atm_blocks, tile_dev, tile_blk, tile_weights, tile_dst, ocean_frac, halo_send):
    myself = lax.axis_index(("gx", "gy"))
    tiles, nodes, cells = tile_weights.shape
    fields_n = atm_blocks.shape[1]
    ocean_n = ocean_frac.shape[0]
    rim_n = halo_send.shape[2]
    source_dev = tile_dev.reshape(DEVICES, tiles)
    block_of = tile_blk.reshape(DEVICES, tiles)
    slots = jnp.arange(CAP, dtype=jnp.int32)
    order = jnp.arange(tiles, dtype=jnp.int32)
    earlier = order[:, None] < order[None, :]
    mine = source_dev == myself
    nth = jnp.dot(mine.astype(jnp.bfloat16), earlier.astype(jnp.bfloat16), preferred_element_type=jnp.float32)
    nth = nth.astype(jnp.int32)
    matched = mine[:, None, :] & (nth[:, None, :] == slots[None, :, None])
    send_blk = jnp.sum(jnp.where(matched, block_of[:, None, :], 0), axis=2).reshape(-1)
    my_source = lax.dynamic_index_in_dim(source_dev, myself, 0, keepdims=False)
    same = (my_source[:, None] == my_source[None, :]) & earlier
    my_nth = jnp.sum(same.astype(jnp.int32), axis=0)
    read_slot = my_source * CAP + my_nth
    slot_range = jnp.arange(DEVICES * CAP, dtype=jnp.int32)
    tile_of = jnp.sum(jnp.where(read_slot[None, :] == slot_range[:, None], order[None, :], 0), axis=1)
    before = (tile_dst[:, None] < tile_dst[None, :]) | ((tile_dst[:, None] == tile_dst[None, :]) & earlier)
    rank = jnp.sum(before.astype(jnp.int32), axis=0)
    placed = rank[None, :] == order[:, None]
    seg_slot = jnp.sum(jnp.where(placed, read_slot[None, :], 0), axis=1)
    seg_dst = jnp.sum(jnp.where(placed, tile_dst[None, :], 0), axis=1)
    seg_keep = jnp.concatenate([jnp.zeros((1,), jnp.int32), (seg_dst[1:] == seg_dst[:-1]).astype(jnp.int32)])
    targets = jnp.arange(ocean_n, dtype=jnp.int32)
    upto = jnp.sum((tile_dst[None, :] <= targets[:, None]).astype(jnp.int32), axis=1)
    any_in = jnp.any(tile_dst[None, :] == targets[:, None], axis=1)
    seg_last = jnp.where(any_in, upto - 1, -1)
    smem = pl.BlockSpec(memory_space=pltpu.SMEM)
    vmem = pl.BlockSpec(memory_space=pltpu.VMEM)
    hbm = pl.BlockSpec(memory_space=pl.ANY)
    block = (fields_n, nodes)
    fields, halo = pl.pallas_call(
        exchange_kernel,
        out_shape=(
            jax.ShapeDtypeStruct((ocean_n, fields_n, cells), jnp.bfloat16),
            jax.ShapeDtypeStruct((2, rim_n, fields_n, cells), jnp.bfloat16),
        ),
        in_specs=[smem] * 6 + [vmem, hbm, vmem],
        out_specs=(hbm, hbm),
        scratch_shapes=[
            pltpu.VMEM(((DEVICES - 1) * CAP,) + block, jnp.bfloat16),
            [pltpu.VMEM((GROUP * CAP,) + block, jnp.bfloat16)] * GROUPS,
            pltpu.VMEM((2 * CAP,) + block, jnp.bfloat16),
            pltpu.VMEM(tile_weights.shape, jnp.bfloat16),
            pltpu.VMEM((DEVICES * CAP, fields_n, cells), jnp.float32),
            pltpu.VMEM((tiles, fields_n, cells), jnp.float32),
            pltpu.VMEM((ocean_n, fields_n, cells), jnp.bfloat16),
            pltpu.VMEM((2 * rim_n, fields_n, cells), jnp.bfloat16),
            pltpu.SemaphoreType.DMA,
            pltpu.SemaphoreType.DMA((GROUPS,)),
            pltpu.SemaphoreType.DMA((2,)),
            pltpu.SemaphoreType.DMA,
            pltpu.SemaphoreType.DMA((2,)),
            pltpu.SemaphoreType.DMA((2,)),
            pltpu.SemaphoreType.DMA,
        ],
        compiler_params=pltpu.CompilerParams(
            collective_id=0, has_side_effects=True, vmem_limit_bytes=56 << 20
        ),
        name="remap_exchange",
    )(
        send_blk, tile_of, seg_slot, seg_keep, seg_last, halo_send.reshape(-1),
        atm_blocks, tile_weights, ocean_frac,
    )
    return fields, halo[None]


def solution(mesh):
    in_specs = (
        P(("gx", "gy"), None, None),
        P(),
        P(),
        P(("gx", "gy"), None, None),
        P(("gx", "gy")),
        P(("gx", "gy"), None),
        P(("gx", "gy"), None, None),
    )
    out_specs = (P(("gx", "gy"), None, None), P(("gx", "gy"), None, None, None, None))
    return jax.shard_map(
        per_device, mesh=mesh, in_specs=in_specs, out_specs=out_specs, check_vma=False
    )
```

time: 186 us -> 127 us (0.68)
  the two profiles are of different devices: /device:TPU:0 before, /device:TPU:10 now
where the time goes in v1:
time: 127 us
  Pallas kernels  106 us (83%)
  local copies, waits for them, and re-layouts  11.3 us (9%)
  other arithmetic  8.12 us (6%)
    pallas_call x1, Pallas kernels, per_device(): pl.pallas_call(exchange_kernel, out_shape=(jax.ShapeDtypeStruct((ocean_n,...  106 us
    unnamed x4, local copies, waits for them, and re-layouts  8.13 us

profile of v1, /device:TPU:10, one launch (start us, length us, event | category | flops | bytes accessed | tf_op | source)
XLA Modules:
  0.0 126.6 jit_solution(8627382477442122447)
XLA Ops:
  0.6 1.3 %reshape.28.halo_idx = s32[16]{0:T(128)} reshape(s32[1,2,8]{2,1,0:T(2,128)} %param.13) | data formatting | bytes 128 | tf_op jit(solution)/shard_map/reshape | solution.py:209
  1.9 0.8 convert_reduce_fusion.2
  2.7 0.8 fusion.4
  3.5 0.6 add_select_fusion.seg_last
  4.1 0.9 convert_reduce_fusion
  5.0 0.5 broadcast.17
  5.5 1.9 %reduce.3 = s32[32768]{0:T(1024)S(1)} reduce(s32[32768,1]{0,1:T(1,128)} %param.8, s32[]{:T(128)} %broadcast.17), dimensions={1}, to_apply=%param.8.reduce_sub_computation.3 | reduce | bytes 262148 | tf_op args[1]
  7.4 0.1 convert_reduce_fusion.1
  7.6 1.4 %select_reduce_fusion.2 = (s32[256]{0:T(256)S(1)}, s32[256]{0:T(256)}) fusion(s32[256]{0:T(256)S(1)} %convert_reduce_fusion, s32[256]{0:T(256)} %param.11, s32[256]{0:T(256)S(1)} %bitcast.7), kind=kLoop, calls=%fused_computation.6 | loop fusion | flops 327168 | bytes 5120 | tf_op jit(solution)/shard_map/reduce_sum | solution.py:169
  9.0 0.1 slice_compare_fusion
  9.1 0.7 add_convert_fusion.seg_keep
  9.7 0.7 select_reduce_fusion.tile_of
  10.5 0.2 convolution_convert_fusion
  10.7 0.9 broadcast_in_dim.45
  11.6 0.2 select_reduce_fusion.1
  11.8 0.1 copy.15
  11.9 0.8 reshape.27.send_blk
  12.7 4.0 %copy.16.atm = bf16[128,30,256]{2,1,0:T(8,128)(2,1)} copy(bf16[128,30,256]{2,0,1:T(8,128)(2,1)} %param.7) | data formatting | bytes 3932160 | tf_op args[0]
  16.7 106.3 %remap_exchange.1 = (bf16[64,30,128]{2,1,0:T(8,128)(2,1)}, bf16[2,8,30,128]{3,2,1,0:T(8,128)(2,1)}) custom-call(s32[384]{0:T(512)} %reshape.27.send_blk, s32[384]{0:T(512)} %select_reduce_fusion.tile_of, s32[256]{0:T(256)} %get-tuple-element.13.seg_slot, s32[256]{0:T(256)} %add_convert_fusion.seg_keep, s32[64]{0:T(128)} %add_select_fusion.seg_last, ...), custom_call_target="tpu_custom_call" | custom-call | tf_op jit(solution)/shard_map/remap_exchange/pallas_call | solution.py:179
  123.0 2.0 %copy.17 = bf16[64,30,128]{2,0,1:T(8,128)(2,1)} copy(bf16[64,30,128]{2,1,0:T(8,128)(2,1)} %get-tuple-element.10) | data formatting | bytes 983040
  125.0 1.6 %copy.18 = bf16[1,2,8,30,128]{4,2,3,1,0:T(8,128)(2,1)} copy(bf16[1,2,8,30,128]{4,3,2,1,0:T(8,128)(2,1)} %bitcast.6) | data formatting | bytes 245760
  (4 shorter events, 0.1 us)

commit v2 on v1

v2 whole, which is shorter than its diff:
```python
import functools

import jax
import jax.numpy as jnp
from jax import lax
from jax.experimental import pallas as pl
from jax.experimental.pallas import tpu as pltpu
from jax.sharding import PartitionSpec as P

MESH = pl.DeviceIdType.MESH
DEVICES = 128
CHIPS = 64
CAP = 3
GROUP = 21
GROUPS = 3
STEPS = GROUP * GROUPS
CORE = 16

SEND, OWN_THIRD, TILE_OF, SEGMENT, UPTO, SHARED = 0, 3, 4, 7, 9, 10
ROWS = 16


def device_index():
    return lax.axis_index("gx") * 16 + lax.axis_index("gy")


def plan_kernel(dev_ref, blk_ref, dst_ref, out_ref):
    n = DEVICES
    myself = device_index()
    lane = lax.broadcasted_iota(jnp.int32, (n, n), 1)
    sub = lax.broadcasted_iota(jnp.int32, (n, n), 0)
    earlier = sub < lane
    halves = [dev_ref[pl.ds(h, n, stride=2), :] for h in (0, 1)]

    full = jnp.zeros((1, n), jnp.int32)
    columns = [half.T for half in halves]
    chips = [((col >> 5) << 4) | (col & 15) for col in columns]
    units = [jnp.left_shift(1, (chip & 7) * 4) for chip in chips]
    for g in range(CHIPS // 8):
        parts = [jnp.where((chip >> 3) == g, unit, 0) for chip, unit in zip(chips, units)]
        counts = jnp.sum(parts[0] + parts[1], axis=0, keepdims=True)
        for j in range(8):
            full = full | (((counts >> (4 * j)) & 15) == 2 * CAP).astype(jnp.int32)
    shared = 1 - jnp.max(full, axis=1, keepdims=True)

    mine = [(half == myself) for half in halves]
    ones = [m.astype(jnp.float32) for m in mine]
    tri = earlier.astype(jnp.bfloat16)
    nth = [jnp.dot(o.astype(jnp.bfloat16), tri, preferred_element_type=jnp.float32) for o in ones]
    first = jnp.sum(ones[0], axis=1, keepdims=True)
    nth[1] = nth[1] + first
    total = first + jnp.sum(ones[1], axis=1, keepdims=True)
    table = jnp.zeros((n, n), jnp.float32)
    for k in range(CAP):
        picked = jnp.zeros((n, 1), jnp.float32)
        for h in (0, 1):
            blocks = blk_ref[pl.ds(h, n, stride=2), :].astype(jnp.float32)
            picked += jnp.sum(jnp.where(mine[h] & (nth[h] == k), blocks, 0.0), axis=1, keepdims=True)
        table = jnp.where(lane == SEND + k, picked, table)
    table = jnp.where(lane == OWN_THIRD, (total >= CAP).astype(jnp.float32), table)
    out_ref[0:8, :] = table.T[0:8, :].astype(jnp.int32)

    def column(row):
        return jnp.broadcast_to(row, (n, n)).T

    src = [dev_ref[pl.ds(2 * myself + h, 1), :] for h in (0, 1)]
    src_col = [column(s) for s in src]

    def count(mask):
        return jnp.sum(mask.astype(jnp.int32), axis=0, keepdims=True)

    place = [
        count((src_col[0] == src[0]) & earlier),
        count(src_col[0] == src[1]) + count((src_col[1] == src[1]) & earlier),
    ]
    slot = []
    for s, p in zip(src, place):
        helper = (s & ~CORE) | (myself & CORE)
        own_chip = (s & ~CORE) == (myself & ~CORE)
        sender = jnp.where((shared == 1) & (p == CAP - 1) & ~own_chip, helper, s)
        slot.append(p * n + sender)
    slot_col = [column(s) for s in slot]
    for k in range(CAP):
        found = jnp.zeros((n, n), jnp.int32)
        for h in (0, 1):
            found += jnp.where(slot_col[h] == lane + k * n, sub + h * n, 0)
        out_ref[TILE_OF + k : TILE_OF + k + 1, :] = jnp.sum(found, axis=0, keepdims=True)

    dst = [dst_ref[h : h + 1, :] for h in (0, 1)]
    key = [d * (2 * n) + lane[0:1] + h * n for h, d in enumerate(dst)]
    key_col = [column(k) for k in key]
    rank = [count(key_col[0] < k) + count(key_col[1] < k) for k in key]
    rank_col = [column(r) for r in rank]
    value_col = [column(s * CHIPS + d) for s, d in zip(slot, dst)]
    for half in (0, 1):
        placed = jnp.zeros((n, n), jnp.int32)
        for h in (0, 1):
            placed += jnp.where(rank_col[h] == lane + half * n, value_col[h], 0)
        out_ref[SEGMENT + half : SEGMENT + half + 1, :] = jnp.sum(placed, axis=0, keepdims=True)
    out_ref[UPTO : UPTO + 1, :] = count(key_col[0] < (lane + 1) * (2 * n)) + count(key_col[1] < (lane + 1) * (2 * n))
    out_ref[SHARED : SHARED + 1, :] = jnp.broadcast_to(shared, (1, n))


def exchange_kernel(
    shared, plan, halo_idx, atm, weights, frac, out_hbm, halo_hbm,
    out_far, out_same, in_far, in_same, lent, borrowed, near, near_out, w_vmem, results, running, fields, rim,
    send_sem, far_sem, same_sem, lend_sem, near_sem, w_sem, rim_send, rim_recv, out_sem,
):
    gx, gy = lax.axis_index("gx"), lax.axis_index("gy")
    myself = gx * 16 + gy
    x, c, y, z = gx // 2, lax.rem(gx, 2), gy // 4, lax.rem(gy, 4)
    other = 1 - c
    far_cap = CAP - 1 if shared else CAP

    def chip_at(i, sign):
        o = lax.rem(i * 37, STEPS) + 1
        cx = lax.rem(x + sign * (o // 16) + 4, 4)
        cy = lax.rem(y + sign * lax.rem(o // 4, 4) + 4, 4)
        cz = lax.rem(z + sign * lax.rem(o, 4) + 4, 4)
        return cx, cy * 4 + cz

    def at(chip, core):
        return chip[0] * 2 + core, chip[1]

    def index(chip, core):
        return chip[0] * 32 + core * 16 + chip[1]

    partner = (x * 2 + other, gy)
    barrier = pltpu.get_barrier_semaphore()
    pl.semaphore_signal(barrier, inc=1, device_id=partner, device_id_type=MESH)

    @pl.loop(0, STEPS)
    def _(i):
        for core in (0, 1):
            pl.semaphore_signal(barrier, inc=1, device_id=at(chip_at(i, 1), core), device_id_type=MESH)

    w_copy = pltpu.make_async_copy(weights, w_vmem, w_sem)
    w_copy.start()

    def block(d, k):
        return atm[plan[SEND + k, d]]

    if shared:

        @pl.loop(0, CHIPS)
        def _(q):
            lent[q] = block(index((q // 16, lax.rem(q, 16)), other), CAP - 1)

    for k in range(CAP):
        near[CAP + k] = block(myself, k)
        near_out[k] = block(index((x, gy), other), k)
    pl.semaphore_wait(barrier, DEVICES - 1)
    if shared:
        lend = pltpu.make_async_remote_copy(
            src_ref=lent, dst_ref=borrowed, send_sem=lend_sem.at[0], recv_sem=lend_sem.at[1],
            device_id=partner, device_id_type=MESH,
        )
        lend.start()
    near_copy = pltpu.make_async_remote_copy(
        src_ref=near_out, dst_ref=near.at[pl.ds(0, CAP)], send_sem=near_sem.at[0], recv_sem=near_sem.at[1],
        device_id=partner, device_id_type=MESH,
    )

    for g in range(GROUPS):

        @pl.loop(0, GROUP)
        def _(j, g=g):
            i = g * GROUP + j
            chip = chip_at(i, 1)
            for k in range(far_cap):
                out_far[i * far_cap + k] = block(index(chip, other), k)
            pltpu.make_async_remote_copy(
                src_ref=out_far.at[pl.ds(i * far_cap, far_cap)],
                dst_ref=in_far[g].at[pl.ds(j * far_cap, far_cap)],
                send_sem=send_sem.at[0], recv_sem=far_sem.at[g],
                device_id=at(chip, other), device_id_type=MESH,
            ).start()

    near_copy.start()
    if shared:
        lend.wait()

    for g in range(GROUPS):

        @pl.loop(0, GROUP)
        def _(j, g=g):
            i = g * GROUP + j
            chip = chip_at(i, 1)
            d = index(chip, c)
            for k in range(far_cap):
                out_same[i * CAP + k] = block(d, k)
            if shared:
                third = block(d, CAP - 1)
                q = chip[0] * 16 + chip[1]
                out_same[i * CAP + CAP - 1] = jnp.where(plan[OWN_THIRD, d] == 1, third, borrowed[q])
            pltpu.make_async_remote_copy(
                src_ref=out_same.at[pl.ds(i * CAP, CAP)],
                dst_ref=in_same[g].at[pl.ds(j * CAP, CAP)],
                send_sem=send_sem.at[1], recv_sem=same_sem.at[g],
                device_id=at(chip, c), device_id_type=MESH,
            ).start()

    w_copy.wait()

    def multiply(buffer, first, s, cap):
        for k in range(cap):
            results[s + DEVICES * k] = jnp.dot(
                buffer[first + k], w_vmem[plan[TILE_OF + k, s]], preferred_element_type=jnp.float32
            )

    multiply(near, CAP, myself, CAP)
    near_copy.wait()
    multiply(near, 0, index((x, gy), other), CAP)
    for buffers, sems, core, cap in ((in_far, far_sem, other, far_cap), (in_same, same_sem, c, CAP)):
        for g in range(GROUPS):
            pltpu.make_async_copy(buffers[g], buffers[g], sems.at[g]).wait()

            @pl.loop(0, GROUP)
            def _(j, g=g, buffers=buffers, core=core, cap=cap):
                multiply(buffers[g], j * cap, index(chip_at(g * GROUP + j, -1), core), cap)

    tiles = running.shape[0]

    def add(r, carry):
        total, previous = carry
        value = plan[SEGMENT + r // DEVICES, lax.rem(r, DEVICES)]
        slot, b = value // CHIPS, lax.rem(value, CHIPS)
        total = total * (b == previous).astype(jnp.float32) + results[slot]
        running[r] = total
        return total, b

    lax.fori_loop(0, tiles, add, (jnp.zeros(running.shape[1:], jnp.float32), jnp.int32(-1)))

    def finish(b, before):
        upto = plan[UPTO, b]
        total = jnp.where(upto > before, running[jnp.maximum(upto - 1, 0)], 0.0)
        fields[b] = (total / frac[pl.ds(b, 1), :]).astype(jnp.bfloat16)
        return upto

    lax.fori_loop(0, fields.shape[0], finish, jnp.int32(0))

    out_copy = pltpu.make_async_copy(fields, out_hbm, out_sem)
    out_copy.start()
    rim_n = rim.shape[0] // 2
    for j in range(2 * rim_n):
        rim[j] = fields[halo_idx[j]]
    up, down = lax.rem(myself + 1, DEVICES), lax.rem(myself + DEVICES - 1, DEVICES)
    rim_copies = []
    for side, there in ((1, up), (0, down)):
        copy = pltpu.make_async_remote_copy(
            src_ref=rim.at[pl.ds(side * rim_n, rim_n)],
            dst_ref=halo_hbm.at[1 - side],
            send_sem=rim_send.at[side],
            recv_sem=rim_recv.at[side],
            device_id=(there // 16, lax.rem(there, 16)),
            device_id_type=MESH,
        )
        copy.start()
        rim_copies.append(copy)
    for copy in rim_copies:
        copy.wait()
    out_copy.wait()
    for which, buffer in enumerate((out_far, out_same)):
        pltpu.make_async_copy(buffer, buffer, send_sem.at[which]).wait()


def exchange(shared, plan, halo_idx, atm, weights, frac):
    tiles, nodes, cells = weights.shape
    fields_n, ocean_n, rim_n = atm.shape[1], frac.shape[0], halo_idx.shape[0] // 2
    smem = pl.BlockSpec(memory_space=pltpu.SMEM)
    vmem = pl.BlockSpec(memory_space=pltpu.VMEM)
    hbm = pl.BlockSpec(memory_space=pl.ANY)
    far_cap = CAP - 1 if shared else CAP
    lent_n = CHIPS if shared else 1

    def blocks(n):
        return pltpu.VMEM((n, fields_n, nodes), jnp.bfloat16)

    return pl.pallas_call(
        functools.partial(exchange_kernel, shared),
        out_shape=(
            jax.ShapeDtypeStruct((ocean_n, fields_n, cells), jnp.bfloat16),
            jax.ShapeDtypeStruct((2, rim_n, fields_n, cells), jnp.bfloat16),
        ),
        in_specs=[smem, smem, vmem, hbm, vmem],
        out_specs=(hbm, hbm),
        scratch_shapes=[
            blocks(STEPS * far_cap),
            blocks(STEPS * CAP),
            [blocks(GROUP * far_cap)] * GROUPS,
            [blocks(GROUP * CAP)] * GROUPS,
            blocks(lent_n),
            blocks(lent_n),
            blocks(2 * CAP),
            blocks(CAP),
            pltpu.VMEM(weights.shape, jnp.bfloat16),
            pltpu.VMEM((DEVICES * CAP, fields_n, cells), jnp.float32),
            pltpu.VMEM((tiles, fields_n, cells), jnp.float32),
            pltpu.VMEM((ocean_n, fields_n, cells), jnp.bfloat16),
            pltpu.VMEM((2 * rim_n, fields_n, cells), jnp.bfloat16),
            pltpu.SemaphoreType.DMA((2,)),
            pltpu.SemaphoreType.DMA((GROUPS,)),
            pltpu.SemaphoreType.DMA((GROUPS,)),
            pltpu.SemaphoreType.DMA((2,)),
            pltpu.SemaphoreType.DMA((2,)),
            pltpu.SemaphoreType.DMA,
            pltpu.SemaphoreType.DMA((2,)),
            pltpu.SemaphoreType.DMA((2,)),
            pltpu.SemaphoreType.DMA,
        ],
        compiler_params=pltpu.CompilerParams(
            collective_id=int(shared), has_side_effects=True, vmem_limit_bytes=56 << 20
        ),
        name="remap_shared" if shared else "remap_direct",
    )(plan, halo_idx, atm, weights, frac)


def per_device(atm_blocks, tile_dev, tile_blk, tile_weights, tile_dst, ocean_frac, halo_send):
    halves = (2 * DEVICES, DEVICES)
    plan = pl.pallas_call(
        plan_kernel,
        out_shape=jax.ShapeDtypeStruct((ROWS, DEVICES), jnp.int32),
        in_specs=[pl.BlockSpec(memory_space=pltpu.VMEM)] * 3,
        out_specs=pl.BlockSpec(memory_space=pltpu.VMEM),
        name="plan",
    )(tile_dev.reshape(halves), tile_blk.reshape(halves), tile_dst.reshape(2, DEVICES))
    fields, halo = lax.cond(
        plan[SHARED, 0] == 1,
        functools.partial(exchange, True),
        functools.partial(exchange, False),
        plan, halo_send.reshape(-1), atm_blocks, tile_weights, ocean_frac,
    )
    return fields, halo[None]


def solution(mesh):
    in_specs = (
        P(("gx", "gy"), None, None),
        P(),
        P(),
        P(("gx", "gy"), None, None),
        P(("gx", "gy")),
        P(("gx", "gy"), None),
        P(("gx", "gy"), None, None),
    )
    out_specs = (P(("gx", "gy"), None, None), P(("gx", "gy"), None, None, None, None))
    return jax.shard_map(
        per_device, mesh=mesh, in_specs=in_specs, out_specs=out_specs, check_vma=False
    )
```

time: 127 us -> 103 us (0.81)
  the two profiles are of different devices: /device:TPU:10 before, /device:TPU:1 now
where the time goes in v2:
time: 103 us
  Pallas kernels  94 us (91%)
  local copies, waits for them, and re-layouts  7.73 us (8%)
  between operations  1.3 us (1%)
    pallas_call x1, Pallas kernels, exchange(): pl.pallas_call(functools.partial(exchange_kernel, shared), out_shape=(jax...  92.3 us
    another operation x1, local copies, waits for them, and re-layouts  4 us

profile of v2, /device:TPU:1, one launch (start us, length us, event | category | flops | bytes accessed | tf_op | source)
XLA Modules:
  0.0 103.1 jit_solution(1612350393752156144)
XLA Ops:
  0.6 1.7 %plan.1 = s32[16,128]{1,0:T(8,128)S(1)} custom-call(s32[256,128]{1,0:T(8,128)} %bitcast.6, s32[256,128]{1,0:T(8,128)} %bitcast.7, s32[2,128]{1,0:T(2,128)} %bitcast.10), custom_call_target="tpu_custom_call" | custom-call | tf_op jit(solution)/shard_map/plan/pallas_call | solution.py:320
  2.4 0.5 slice.4
  3.5 98.6 %conditional.1 = (bf16[64,30,128]{2,1,0:T(8,128)(2,1)S(1)}, bf16[1,2,8,30,128]{4,2,3,1,0:T(8,128)(2,1)S(1)}) conditional(s32[]{:T(128)} %bitcast.5, (s32[1,2,8]{2,1,0:T(2,128)}, s32[16,128]{1,0:T(8,128)S(1)}, bf16[128,30,256]{2,0,1:T(8,128)(2,1)}, bf16[256,256,128]{2,1,0:T(8,128)(2,1)}, f32[64,128]{1,0:T(8,128)}) %tuple.17, (s32[1,2,8]{2,1,0:T(2,128)}, ...), branch_computations={%region_0.0_spmd, %region_1.0_spmd} | conditional | bytes 4309164 | solution.py:327
  3.6 0.0 copy-start.1
  3.6 1.3 %reshape.20.halo_idx = s32[16]{0:T(128)} reshape(s32[1,2,8]{2,1,0:T(2,128)} %get-tuple-element.53) | data formatting | bytes 128 | tf_op jit(solution)/shard_map/reshape | solution.py:331
  4.8 4.0 %copy.20.atm = bf16[128,30,256]{2,1,0:T(8,128)(2,1)} copy(bf16[128,30,256]{2,0,1:T(8,128)(2,1)} %get-tuple-element.67) | data formatting | bytes 3932160 | tf_op jit(solution)/shard_map
  8.9 0.0 copy-done.1
  8.9 92.3 %remap_shared.1 = (bf16[64,30,128]{2,1,0:T(8,128)(2,1)S(1)}, bf16[2,8,30,128]{3,2,1,0:T(8,128)(2,1)}) custom-call(s32[16,128]{1,0:T(8,128)S(1)} %get-tuple-element.34.plan, s32[16]{0:T(128)} %reshape.20.halo_idx, bf16[128,30,256]{2,1,0:T(8,128)(2,1)} %copy.20.atm, bf16[256,256,128]{2,1,0:T(8,128)(2,1)} %get-tuple-element.57.weights, f32[64,128]{1,0:T(8,128)S(1)} %copy-done.1), custom_call_target="tpu_custom_call" | custom-call | tf_op jit(solution)/shard_map/cond/branch_1_fun/remap_shared/pallas_call | solution.py:279
  101.2 1.0 copy.24
  102.1 0.0 copy-start.2
  102.1 1.0 copy.21
  103.1 0.0 copy-done.2
Async XLA Ops:
  3.6 5.3 %copy-start.1 = (f32[64,128]{1,0:T(8,128)S(1)}, f32[64,128]{1,0:T(8,128)}, u32[]{:S(2)}) copy-start(f32[64,128]{1,0:T(8,128)} %get-tuple-element.59.frac) | copy-start | bytes 98308 | tf_op jit(solution)/shard_map/cond
  102.1 1.0 copy-start.2

commit v3 on v2

--- a/solution.py
+++ b/solution.py
@@ -11,12 +11,12 @@
 DEVICES = 128
 CHIPS = 64
 CAP = 3
-GROUP = 21
-GROUPS = 3
-STEPS = GROUP * GROUPS
+STEPS = 63
+FAR_GROUPS = (21, 21, 21)
+SAME_GROUPS = (21, 21, 14, 7)
 CORE = 16
 
-SEND, OWN_THIRD, TILE_OF, SEGMENT, UPTO, SHARED = 0, 3, 4, 7, 9, 10
+SEND, OWN_THIRD, TILE_OF, SEGMENT, UPTO = 0, 3, 4, 7, 9
 ROWS = 16
 
 
@@ -24,7 +24,7 @@
     return lax.axis_index("gx") * 16 + lax.axis_index("gy")
 
 
-def plan_kernel(dev_ref, blk_ref, dst_ref, out_ref):
+def plan_kernel(dev_ref, blk_ref, dst_ref, out_ref, shared_ref):
     n = DEVICES
     myself = device_index()
     lane = lax.broadcasted_iota(jnp.int32, (n, n), 1)
@@ -98,12 +98,12 @@
             placed += jnp.where(rank_col[h] == lane + half * n, value_col[h], 0)
         out_ref[SEGMENT + half : SEGMENT + half + 1, :] = jnp.sum(placed, axis=0, keepdims=True)
     out_ref[UPTO : UPTO + 1, :] = count(key_col[0] < (lane + 1) * (2 * n)) + count(key_col[1] < (lane + 1) * (2 * n))
-    out_ref[SHARED : SHARED + 1, :] = jnp.broadcast_to(shared, (1, n))
+    shared_ref[0] = jnp.max(shared)
 
 
 def exchange_kernel(
-    shared, plan, halo_idx, atm, weights, frac, out_hbm, halo_hbm,
-    out_far, out_same, in_far, in_same, lent, borrowed, near, near_out, w_vmem, results, running, fields, rim,
+    shared, plan, halo_idx, atm_by_field, weights, frac, out_hbm, halo_hbm,
+    atm, out_far, out_same, in_far, in_same, lent, borrowed, near, near_out, w_vmem, results, running, fields, rim,
     send_sem, far_sem, same_sem, lend_sem, near_sem, w_sem, rim_send, rim_recv, out_sem,
 ):
     gx, gy = lax.axis_index("gx"), lax.axis_index("gy")
@@ -137,8 +137,28 @@
     w_copy = pltpu.make_async_copy(weights, w_vmem, w_sem)
     w_copy.start()
 
+    rows = 16
+
+    @pl.loop(0, atm.shape[0] // rows)
+    def _(i):
+        part = pl.ds(pl.multiple_of(i * rows, rows), rows)
+        atm[part] = jnp.swapaxes(atm_by_field[:, part, :], 0, 1)
+
     def block(d, k):
         return atm[plan[SEND + k, d]]
+
+    f = atm.shape[1]
+    half = atm.shape[2] // 2
+
+    def pack(blocks):
+        parts = []
+        for b in blocks:
+            parts += [b[:, :half], b[:, half:]]
+        return jnp.concatenate(parts, axis=0)
+
+    def unpack(buffer, j, k):
+        parts = [buffer[j, pl.ds((2 * k + h) * f, f), :] for h in (0, 1)]
+        return jnp.concatenate(parts, axis=1)
 
     if shared:
 
@@ -161,63 +181,72 @@
         device_id=partner, device_id_type=MESH,
     )
 
-    for g in range(GROUPS):
-
-        @pl.loop(0, GROUP)
-        def _(j, g=g):
-            i = g * GROUP + j
+    start = 0
+    for g, size in enumerate(FAR_GROUPS):
+
+        @pl.loop(0, size)
+        def _(j, g=g, start=start):
+            i = start + j
             chip = chip_at(i, 1)
-            for k in range(far_cap):
-                out_far[i * far_cap + k] = block(index(chip, other), k)
+            d = index(chip, other)
+            out_far[i] = pack([block(d, k) for k in range(far_cap)])
             pltpu.make_async_remote_copy(
-                src_ref=out_far.at[pl.ds(i * far_cap, far_cap)],
-                dst_ref=in_far[g].at[pl.ds(j * far_cap, far_cap)],
+                src_ref=out_far.at[i], dst_ref=in_far[g].at[j],
                 send_sem=send_sem.at[0], recv_sem=far_sem.at[g],
                 device_id=at(chip, other), device_id_type=MESH,
             ).start()
 
+        start += size
+
     near_copy.start()
     if shared:
         lend.wait()
 
-    for g in range(GROUPS):
-
-        @pl.loop(0, GROUP)
-        def _(j, g=g):
-            i = g * GROUP + j
+    start = 0
+    for g, size in enumerate(SAME_GROUPS):
+
+        @pl.loop(0, size)
+        def _(j, g=g, start=start):
+            i = start + j
             chip = chip_at(i, 1)
             d = index(chip, c)
-            for k in range(far_cap):
-                out_same[i * CAP + k] = block(d, k)
+            blocks = [block(d, k) for k in range(CAP)]
             if shared:
-                third = block(d, CAP - 1)
                 q = chip[0] * 16 + chip[1]
-                out_same[i * CAP + CAP - 1] = jnp.where(plan[OWN_THIRD, d] == 1, third, borrowed[q])
+                blocks[-1] = jnp.where(plan[OWN_THIRD, d] == 1, blocks[-1], borrowed[q])
+            out_same[i] = pack(blocks)
             pltpu.make_async_remote_copy(
-                src_ref=out_same.at[pl.ds(i * CAP, CAP)],
-                dst_ref=in_same[g].at[pl.ds(j * CAP, CAP)],
+                src_ref=out_same.at[i], dst_ref=in_same[g].at[j],
                 send_sem=send_sem.at[1], recv_sem=same_sem.at[g],
                 device_id=at(chip, c), device_id_type=MESH,
             ).start()
 
+        start += size
+
     w_copy.wait()
 
-    def multiply(buffer, first, s, cap):
-        for k in range(cap):
+    def multiply(s, blocks):
+        for k, b in enumerate(blocks):
             results[s + DEVICES * k] = jnp.dot(
-                buffer[first + k], w_vmem[plan[TILE_OF + k, s]], preferred_element_type=jnp.float32
+                b, w_vmem[plan[TILE_OF + k, s]], preferred_element_type=jnp.float32
             )
 
-    multiply(near, CAP, myself, CAP)
+    multiply(myself, [near[CAP + k] for k in range(CAP)])
     near_copy.wait()
-    multiply(near, 0, index((x, gy), other), CAP)
-    for buffers, sems, core, cap in ((in_far, far_sem, other, far_cap), (in_same, same_sem, c, CAP)):
-        for g in range(GROUPS):
+    multiply(index((x, gy), other), [near[k] for k in range(CAP)])
+    for buffers, sems, sizes, core, cap in (
+        (in_far, far_sem, FAR_GROUPS, other, far_cap),
+        (in_same, same_sem, SAME_GROUPS, c, CAP),
+    ):
+        start = 0
+        for g, size in enumerate(sizes):
             pltpu.make_async_copy(buffers[g], buffers[g], sems.at[g]).wait()
 
-            @pl.loop(0, GROUP)
-            def _(j, g=g, buffers=buffers, core=core, cap=cap):
-                multiply(buffers[g], j * cap, index(chip_at(g * GROUP + j, -1), core), cap)
+            @pl.loop(0, size)
+            def _(j, buffer=buffers[g], start=start, core=core, cap=cap):
+                multiply(index(chip_at(start + j, -1), core), [unpack(buffer, j, k) for k in range(cap)])
+
+            start += size
 
     tiles = running.shape[0]
 
@@ -229,21 +258,18 @@
         running[r] = total
         return total, b
 
-    lax.fori_loop(0, tiles, add, (jnp.zeros(running.shape[1:], jnp.float32), jnp.int32(-1)))
-
-    def finish(b, before):
+    lax.fori_loop(0, tiles, add, (jnp.zeros(running.shape[1:], jnp.float32), jnp.int32(-1)), unroll=8)
+
+    def finished(b):
         upto = plan[UPTO, b]
+        before = jnp.where(b > 0, plan[UPTO, jnp.maximum(b - 1, 0)], 0)
         total = jnp.where(upto > before, running[jnp.maximum(upto - 1, 0)], 0.0)
-        fields[b] = (total / frac[pl.ds(b, 1), :]).astype(jnp.bfloat16)
-        return upto
-
-    lax.fori_loop(0, fields.shape[0], finish, jnp.int32(0))
-
-    out_copy = pltpu.make_async_copy(fields, out_hbm, out_sem)
-    out_copy.start()
+        return (total / frac[pl.ds(b, 1), :]).astype(jnp.bfloat16)
+
     rim_n = rim.shape[0] // 2
-    for j in range(2 * rim_n):
-        rim[j] = fields[halo_idx[j]]
+    for side in (0, 1):
+        for j in range(rim_n):
+            rim[side * rim_n + j] = finished(halo_idx[side, j])
     up, down = lax.rem(myself + 1, DEVICES), lax.rem(myself + DEVICES - 1, DEVICES)
     rim_copies = []
     for side, there in ((1, up), (0, down)):
@@ -257,6 +283,13 @@
         )
         copy.start()
         rim_copies.append(copy)
+
+    @pl.loop(0, fields.shape[0], unroll=4)
+    def _(b):
+        fields[b] = finished(b)
+
+    out_copy = pltpu.make_async_copy(fields, out_hbm, out_sem)
+    out_copy.start()
     for copy in rim_copies:
         copy.wait()
     out_copy.wait()
@@ -264,9 +297,10 @@
         pltpu.make_async_copy(buffer, buffer, send_sem.at[which]).wait()
 
 
-def exchange(shared, plan, halo_idx, atm, weights, frac):
+def exchange(shared, plan, halo_idx, atm_by_field, weights, frac):
     tiles, nodes, cells = weights.shape
-    fields_n, ocean_n, rim_n = atm.shape[1], frac.shape[0], halo_idx.shape[0] // 2
+    fields_n, blocks_n = atm_by_field.shape[:2]
+    ocean_n, rim_n = frac.shape[0], halo_idx.shape[1]
     smem = pl.BlockSpec(memory_space=pltpu.SMEM)
     vmem = pl.BlockSpec(memory_space=pltpu.VMEM)
     hbm = pl.BlockSpec(memory_space=pl.ANY)
@@ -275,6 +309,9 @@
 
     def blocks(n):
         return pltpu.VMEM((n, fields_n, nodes), jnp.bfloat16)
+
+    def messages(n, cap):
+        return pltpu.VMEM((n, cap * 2 * fields_n, nodes // 2), jnp.bfloat16)
 
     return pl.pallas_call(
         functools.partial(exchange_kernel, shared),
@@ -285,10 +322,11 @@
         in_specs=[smem, smem, vmem, hbm, vmem],
         out_specs=(hbm, hbm),
         scratch_shapes=[
-            blocks(STEPS * far_cap),
-            blocks(STEPS * CAP),
-            [blocks(GROUP * far_cap)] * GROUPS,
-            [blocks(GROUP * CAP)] * GROUPS,
+            blocks(blocks_n),
+            messages(STEPS, far_cap),
+            messages(STEPS, CAP),
+            [messages(n, far_cap) for n in FAR_GROUPS],
+            [messages(n, CAP) for n in SAME_GROUPS],
             blocks(lent_n),
             blocks(lent_n),
             blocks(2 * CAP),
@@ -299,8 +337,8 @@
             pltpu.VMEM((ocean_n, fields_n, cells), jnp.bfloat16),
             pltpu.VMEM((2 * rim_n, fields_n, cells), jnp.bfloat16),
             pltpu.SemaphoreType.DMA((2,)),
-            pltpu.SemaphoreType.DMA((GROUPS,)),
-            pltpu.SemaphoreType.DMA((GROUPS,)),
+            pltpu.SemaphoreType.DMA((len(FAR_GROUPS),)),
+            pltpu.SemaphoreType.DMA((len(SAME_GROUPS),)),
             pltpu.SemaphoreType.DMA((2,)),
             pltpu.SemaphoreType.DMA((2,)),
             pltpu.SemaphoreType.DMA,
@@ -312,23 +350,23 @@
             collective_id=int(shared), has_side_effects=True, vmem_limit_bytes=56 << 20
         ),
         name="remap_shared" if shared else "remap_direct",
-    )(plan, halo_idx, atm, weights, frac)
+    )(plan, halo_idx, atm_by_field, weights, frac)
 
 
 def per_device(atm_blocks, tile_dev, tile_blk, tile_weights, tile_dst, ocean_frac, halo_send):
     halves = (2 * DEVICES, DEVICES)
-    plan = pl.pallas_call(
+    plan, shared = pl.pallas_call(
         plan_kernel,
-        out_shape=jax.ShapeDtypeStruct((ROWS, DEVICES), jnp.int32),
+        out_shape=(jax.ShapeDtypeStruct((ROWS, DEVICES), jnp.int32), jax.ShapeDtypeStruct((1,), jnp.int32)),
         in_specs=[pl.BlockSpec(memory_space=pltpu.VMEM)] * 3,
-        out_specs=pl.BlockSpec(memory_space=pltpu.VMEM),
+        out_specs=(pl.BlockSpec(memory_space=pltpu.VMEM), pl.BlockSpec(memory_space=pltpu.SMEM)),
         name="plan",
     )(tile_dev.reshape(halves), tile_blk.reshape(halves), tile_dst.reshape(2, DEVICES))
     fields, halo = lax.cond(
-        plan[SHARED, 0] == 1,
+        shared.reshape(()) == 1,
         functools.partial(exchange, True),
         functools.partial(exchange, False),
-        plan, halo_send.reshape(-1), atm_blocks, tile_weights, ocean_frac,
+        plan, halo_send[0], jnp.swapaxes(atm_blocks, 0, 1), tile_weights, ocean_frac,
     )
     return fields, halo[None]
 

time: 103 us -> 109 us (1.058); the launches traced: 103 us -> 108 us
  Pallas kernels: 94 us -> 105 us
  local copies, waits for them, and re-layouts: 7.73 us -> 1.93 us
    pallas_call x1, Pallas kernels: 92.3 us -> 103 us  [exchange(): pl.pallas_call(functools.partial(exchange_kernel, shared), out_shape=(jax...]
    another operation x1 -> x0, local copies, waits for them, and re-layouts: 4 us -> none
    reshape x1 -> x0, local copies, waits for them, and re-layouts: 1.27 us -> none  [per_device(): halo_send.reshape(-1)]
where the time goes in v3:
time: 109 us; the launch traced here: 108 us
  Pallas kernels  105 us (96%)
  local copies, waits for them, and re-layouts  1.93 us (2%)
  between operations  1.3 us (1%)
    pallas_call x1, Pallas kernels, exchange(): pl.pallas_call(functools.partial(exchange_kernel, shared), out_shape=(jax...  103 us

profile of v3, /device:TPU:1, one launch (start us, length us, event | category | flops | bytes accessed | tf_op | source)
XLA Modules:
  0.0 107.8 jit_solution(4387353072525668892)
XLA Ops:
  0.6 2.0 %plan.1 = (s32[16,128]{1,0:T(8,128)S(1)}, s32[1]{0:T(128)}) custom-call(s32[256,128]{1,0:T(8,128)} %bitcast.11, s32[256,128]{1,0:T(8,128)} %bitcast.12, s32[2,128]{1,0:T(2,128)} %bitcast.17), custom_call_target="tpu_custom_call" | custom-call | tf_op jit(solution)/shard_map/plan/pallas_call | solution.py:358
  3.3 103.5 %conditional.1 = (bf16[64,30,128]{2,1,0:T(8,128)(2,1)S(1)}, bf16[1,2,8,30,128]{4,2,3,1,0:T(8,128)(2,1)S(1)}) conditional(s32[]{:T(128)} %bitcast.7, (s32[1,2,8]{2,1,0:T(2,128)}, s32[16,128]{1,0:T(8,128)S(1)}, bf16[30,128,256]{2,1,0:T(8,128)(2,1)}, bf16[256,256,128]{2,1,0:T(8,128)(2,1)}, f32[64,128]{1,0:T(8,128)}) %tuple.25, (s32[1,2,8]{2,1,0:T(2,128)}, ...), branch_computations={%region_0.0_spmd, %region_1.0_spmd} | conditional | bytes 245776 | solution.py:365
  3.3 102.5 %remap_direct.1 = (bf16[64,30,128]{2,1,0:T(8,128)(2,1)S(1)}, bf16[2,8,30,128]{3,2,1,0:T(8,128)(2,1)}) custom-call(s32[16,128]{1,0:T(8,128)S(1)} %get-tuple-element.27.plan, s32[2,8]{1,0:T(2,128)} %bitcast.15, bf16[30,128,256]{2,1,0:T(8,128)(2,1)} %get-tuple-element.29.atm_by_field, bf16[256,256,128]{2,1,0:T(8,128)(2,1)} %get-tuple-element.56.weights, ...), custom_call_target="tpu_custom_call" | custom-call | tf_op jit(solution)/shard_map/cond/branch_0_fun/remap_direct/pallas_call | solution.py:316
  105.8 1.0 copy.19
  106.8 0.0 copy-start
  106.8 1.0 copy.17
  107.8 0.0 copy-done
Async XLA Ops:
  106.8 1.0 copy-start

commit v4 on v3

--- a/solution.py
+++ b/solution.py
@@ -12,8 +12,7 @@
 CHIPS = 64
 CAP = 3
 STEPS = 63
-FAR_GROUPS = (21, 21, 21)
-SAME_GROUPS = (21, 21, 14, 7)
+STRIDE = 29
 CORE = 16
 
 SEND, OWN_THIRD, TILE_OF, SEGMENT, UPTO = 0, 3, 4, 7, 9
@@ -113,7 +112,7 @@
     far_cap = CAP - 1 if shared else CAP
 
     def chip_at(i, sign):
-        o = lax.rem(i * 37, STEPS) + 1
+        o = lax.rem(i * STRIDE, STEPS) + 1
         cx = lax.rem(x + sign * (o // 16) + 4, 4)
         cy = lax.rem(y + sign * lax.rem(o // 4, 4) + 4, 4)
         cz = lax.rem(z + sign * lax.rem(o, 4) + 4, 4)
@@ -181,49 +180,27 @@
         device_id=partner, device_id_type=MESH,
     )
 
-    start = 0
-    for g, size in enumerate(FAR_GROUPS):
-
-        @pl.loop(0, size)
-        def _(j, g=g, start=start):
-            i = start + j
-            chip = chip_at(i, 1)
-            d = index(chip, other)
-            out_far[i] = pack([block(d, k) for k in range(far_cap)])
-            pltpu.make_async_remote_copy(
-                src_ref=out_far.at[i], dst_ref=in_far[g].at[j],
-                send_sem=send_sem.at[0], recv_sem=far_sem.at[g],
-                device_id=at(chip, other), device_id_type=MESH,
-            ).start()
-
-        start += size
-
-    near_copy.start()
-    if shared:
-        lend.wait()
-
-    start = 0
-    for g, size in enumerate(SAME_GROUPS):
-
-        @pl.loop(0, size)
-        def _(j, g=g, start=start):
-            i = start + j
-            chip = chip_at(i, 1)
-            d = index(chip, c)
-            blocks = [block(d, k) for k in range(CAP)]
-            if shared:
-                q = chip[0] * 16 + chip[1]
-                blocks[-1] = jnp.where(plan[OWN_THIRD, d] == 1, blocks[-1], borrowed[q])
-            out_same[i] = pack(blocks)
-            pltpu.make_async_remote_copy(
-                src_ref=out_same.at[i], dst_ref=in_same[g].at[j],
-                send_sem=send_sem.at[1], recv_sem=same_sem.at[g],
-                device_id=at(chip, c), device_id_type=MESH,
-            ).start()
-
-        start += size
-
-    w_copy.wait()
+    def send_far(i):
+        chip = chip_at(i, 1)
+        d = index(chip, other)
+        out_far[i] = pack([block(d, k) for k in range(far_cap)])
+        pltpu.make_async_remote_copy(
+            src_ref=out_far.at[i], dst_ref=in_far.at[i], send_sem=send_sem.at[0], recv_sem=far_sem.at[i],
+            device_id=at(chip, other), device_id_type=MESH,
+        ).start()
+
+    def send_same(i):
+        chip = chip_at(i, 1)
+        d = index(chip, c)
+        blocks = [block(d, k) for k in range(CAP)]
+        if shared:
+            q = chip[0] * 16 + chip[1]
+            blocks[-1] = jnp.where(plan[OWN_THIRD, d] == 1, blocks[-1], borrowed[q])
+        out_same[i] = pack(blocks)
+        pltpu.make_async_remote_copy(
+            src_ref=out_same.at[i], dst_ref=in_same.at[i], send_sem=send_sem.at[1], recv_sem=same_sem.at[i],
+            device_id=at(chip, c), device_id_type=MESH,
+        ).start()
 
     def multiply(s, blocks):
         for k, b in enumerate(blocks):
@@ -231,50 +208,82 @@
                 b, w_vmem[plan[TILE_OF + k, s]], preferred_element_type=jnp.float32
             )
 
+    def wait_far(i):
+        pltpu.make_async_copy(in_far.at[i], in_far.at[i], far_sem.at[i]).wait()
+
+    def wait_same(i):
+        pltpu.make_async_copy(in_same.at[i], in_same.at[i], same_sem.at[i]).wait()
+
+    def take_far(i):
+        multiply(index(chip_at(i, -1), other), [unpack(in_far, i, k) for k in range(far_cap)])
+
+    def take_same(i):
+        multiply(index(chip_at(i, -1), c), [unpack(in_same, i, k) for k in range(CAP)])
+
+    @pl.loop(0, STEPS)
+    def _(i):
+        send_far(i)
+
+    near_copy.start()
+    if shared:
+        lend.wait()
+
+    @pl.loop(0, STEPS)
+    def _(i):
+        send_same(i)
+
+    w_copy.wait()
     multiply(myself, [near[CAP + k] for k in range(CAP)])
     near_copy.wait()
     multiply(index((x, gy), other), [near[k] for k in range(CAP)])
-    for buffers, sems, sizes, core, cap in (
-        (in_far, far_sem, FAR_GROUPS, other, far_cap),
-        (in_same, same_sem, SAME_GROUPS, c, CAP),
-    ):
-        start = 0
-        for g, size in enumerate(sizes):
-            pltpu.make_async_copy(buffers[g], buffers[g], sems.at[g]).wait()
-
-            @pl.loop(0, size)
-            def _(j, buffer=buffers[g], start=start, core=core, cap=cap):
-                multiply(index(chip_at(start + j, -1), core), [unpack(buffer, j, k) for k in range(cap)])
-
-            start += size
-
-    tiles = running.shape[0]
+
+    @pl.loop(0, STEPS // 7)
+    def _(g):
+        for j in range(7):
+            wait_far(g * 7 + j)
+        for j in range(7):
+            take_far(g * 7 + j)
+
+    @pl.loop(0, STEPS // 7)
+    def _(g):
+        for j in range(7):
+            wait_same(g * 7 + j)
+        for j in range(7):
+            take_same(g * 7 + j)
+
+    middle = running.shape[0] // 2
 
     def add(r, carry):
-        total, previous = carry
-        value = plan[SEGMENT + r // DEVICES, lax.rem(r, DEVICES)]
-        slot, b = value // CHIPS, lax.rem(value, CHIPS)
-        total = total * (b == previous).astype(jnp.float32) + results[slot]
-        running[r] = total
-        return total, b
-
-    lax.fori_loop(0, tiles, add, (jnp.zeros(running.shape[1:], jnp.float32), jnp.int32(-1)), unroll=8)
+        new = []
+        for (total, previous), at_r in zip(carry, (r, r + middle)):
+            value = plan[SEGMENT + at_r // DEVICES, lax.rem(at_r, DEVICES)]
+            slot, b = value // CHIPS, lax.rem(value, CHIPS)
+            total = jnp.where(b == previous, total, 0.0) + results[slot]
+            running[at_r] = total
+            new.append((total, b))
+        return tuple(new)
+
+    none = (jnp.zeros(running.shape[1:], jnp.float32), jnp.int32(-1))
+    lax.fori_loop(0, middle, add, (none, none), unroll=4)
 
     def finished(b):
         upto = plan[UPTO, b]
         before = jnp.where(b > 0, plan[UPTO, jnp.maximum(b - 1, 0)], 0)
         total = jnp.where(upto > before, running[jnp.maximum(upto - 1, 0)], 0.0)
-        return (total / frac[pl.ds(b, 1), :]).astype(jnp.bfloat16)
-
-    rim_n = rim.shape[0] // 2
+        total += jnp.where((before < middle) & (upto > middle), running[middle - 1], 0.0)
+        return total / frac[pl.ds(b, 1), :]
+
+    def by_field(blocks):
+        return jnp.swapaxes(jnp.stack(blocks), 0, 1).astype(jnp.bfloat16)
+
+    rim_n = rim.shape[2]
     for side in (0, 1):
-        for j in range(rim_n):
-            rim[side * rim_n + j] = finished(halo_idx[side, j])
+        rim[side] = by_field([finished(halo_idx[side, j]) for j in range(rim_n)])
     up, down = lax.rem(myself + 1, DEVICES), lax.rem(myself + DEVICES - 1, DEVICES)
     rim_copies = []
     for side, there in ((1, up), (0, down)):
         copy = pltpu.make_async_remote_copy(
-            src_ref=rim.at[pl.ds(side * rim_n, rim_n)],
+            src_ref=rim.at[side],
             dst_ref=halo_hbm.at[1 - side],
             send_sem=rim_send.at[side],
             recv_sem=rim_recv.at[side],
@@ -284,9 +293,10 @@
         copy.start()
         rim_copies.append(copy)
 
-    @pl.loop(0, fields.shape[0], unroll=4)
-    def _(b):
-        fields[b] = finished(b)
+    @pl.loop(0, fields.shape[1] // rows)
+    def _(i):
+        first = pl.multiple_of(i * rows, rows)
+        fields[:, pl.ds(first, rows), :] = by_field([finished(first + j) for j in range(rows)])
 
     out_copy = pltpu.make_async_copy(fields, out_hbm, out_sem)
     out_copy.start()
@@ -316,8 +326,8 @@
     return pl.pallas_call(
         functools.partial(exchange_kernel, shared),
         out_shape=(
-            jax.ShapeDtypeStruct((ocean_n, fields_n, cells), jnp.bfloat16),
-            jax.ShapeDtypeStruct((2, rim_n, fields_n, cells), jnp.bfloat16),
+            jax.ShapeDtypeStruct((fields_n, ocean_n, cells), jnp.bfloat16),
+            jax.ShapeDtypeStruct((2, fields_n, rim_n, cells), jnp.bfloat16),
         ),
         in_specs=[smem, smem, vmem, hbm, vmem],
         out_specs=(hbm, hbm),
@@ -325,8 +335,8 @@
             blocks(blocks_n),
             messages(STEPS, far_cap),
             messages(STEPS, CAP),
-            [messages(n, far_cap) for n in FAR_GROUPS],
-            [messages(n, CAP) for n in SAME_GROUPS],
+            messages(STEPS, far_cap),
+            messages(STEPS, CAP),
             blocks(lent_n),
             blocks(lent_n),
             blocks(2 * CAP),
@@ -334,11 +344,11 @@
             pltpu.VMEM(weights.shape, jnp.bfloat16),
             pltpu.VMEM((DEVICES * CAP, fields_n, cells), jnp.float32),
             pltpu.VMEM((tiles, fields_n, cells), jnp.float32),
-            pltpu.VMEM((ocean_n, fields_n, cells), jnp.bfloat16),
-            pltpu.VMEM((2 * rim_n, fields_n, cells), jnp.bfloat16),
-            pltpu.SemaphoreType.DMA((2,)),
-            pltpu.SemaphoreType.DMA((len(FAR_GROUPS),)),
-            pltpu.SemaphoreType.DMA((len(SAME_GROUPS),)),
+            pltpu.VMEM((fields_n, ocean_n, cells), jnp.bfloat16),
+            pltpu.VMEM((2, fields_n, rim_n, cells), jnp.bfloat16),
+            pltpu.SemaphoreType.DMA((2,)),
+            pltpu.SemaphoreType.DMA((STEPS,)),
+            pltpu.SemaphoreType.DMA((STEPS,)),
             pltpu.SemaphoreType.DMA((2,)),
             pltpu.SemaphoreType.DMA((2,)),
             pltpu.SemaphoreType.DMA,
@@ -368,7 +378,7 @@
         functools.partial(exchange, False),
         plan, halo_send[0], jnp.swapaxes(atm_blocks, 0, 1), tile_weights, ocean_frac,
     )
-    return fields, halo[None]
+    return jnp.swapaxes(fields, 0, 1), jnp.swapaxes(halo, 1, 2)[None]
 
 
 def solution(mesh):

time: 109 us -> 86.7 us (0.80)
  Pallas kernels: 105 us -> 83.8 us
    pallas_call x1, Pallas kernels: 103 us -> 81.8 us  [exchange(): pl.pallas_call(functools.partial(exchange_kernel, shared), out_shape=(jax...]
    cond x2 -> x0, local copies, waits for them, and re-layouts: 1.93 us -> none  [per_device(): lax.cond(shared.reshape(()) == 1, functools.partial(exchange, True), func...]
    unnamed x2, local copies, waits for them, and re-layouts: 0.01 us -> 1.43 us
where the time goes in v4:
time: 86.7 us; the launch traced here: 86.6 us
  Pallas kernels  83.8 us (97%)
  local copies, waits for them, and re-layouts  1.43 us (2%)
  between operations  1.3 us (1%)
    pallas_call x1, Pallas kernels, exchange(): pl.pallas_call(functools.partial(exchange_kernel, shared), out_shape=(jax...  81.8 us
    pallas_call x1, Pallas kernels, per_device(): pl.pallas_call(plan_kernel, out_shape=(jax.ShapeDtypeStruct((ROWS, DEVICE...  2 us

profile of v4, /device:TPU:1, one launch (start us, length us, event | category | flops | bytes accessed | tf_op | source)
XLA Modules:
  0.0 86.6 jit_solution(9125093957115096932)
XLA Ops:
  0.6 2.0 %plan.1 = (s32[16,128]{1,0:T(8,128)S(1)}, s32[1]{0:T(128)}) custom-call(s32[256,128]{1,0:T(8,128)} %bitcast.13, s32[256,128]{1,0:T(8,128)} %bitcast.14, s32[2,128]{1,0:T(2,128)} %bitcast.18), custom_call_target="tpu_custom_call" | custom-call | tf_op jit(solution)/shard_map/plan/pallas_call | solution.py:368
  3.3 81.8 %conditional.1 = ((bf16[30,64,128]{2,1,0:T(8,128)(2,1)S(1)}, bf16[2,30,8,128]{3,2,1,0:T(8,128)(2,1)S(1)})) conditional(s32[]{:T(128)} %bitcast.3, (s32[16,128]{1,0:T(8,128)S(1)}, s32[2,8]{1,0:T(2,128)}, bf16[30,128,256]{2,1,0:T(8,128)(2,1)}, bf16[256,256,128]{2,1,0:T(8,128)(2,1)}, f32[64,128]{1,0:T(8,128)}) %tuple.24, (s32[16,128]{1,0:T(8,128)S(1)}, ...), branch_computations={%region_0.0_spmd, %region_1.0_spmd} | conditional | bytes 8 | solution.py:375
  3.3 81.8 %remap_shared.1 = (bf16[30,64,128]{2,1,0:T(8,128)(2,1)S(1)}, bf16[2,30,8,128]{3,2,1,0:T(8,128)(2,1)S(1)}) custom-call(s32[16,128]{1,0:T(8,128)S(1)} %get-tuple-element.25.plan, s32[2,8]{1,0:T(2,128)} %get-tuple-element.26.halo_idx, bf16[30,128,256]{2,1,0:T(8,128)(2,1)} %get-tuple-element.27.atm_by_field, bf16[256,256,128]{2,1,0:T(8,128)(2,1)} %get-tuple-element.28.weights, ...), custom_call_target="tpu_custom_call" | custom-call | tf_op jit(solution)/shard_map/cond/branch_1_fun/remap_shared/pallas_call | solution.py:326
  85.1 0.8 copy.15
  85.9 0.6 copy.16

commit v5 on v4

--- a/solution.py
+++ b/solution.py
@@ -255,16 +255,16 @@
 
     def add(r, carry):
         new = []
-        for (total, previous), at_r in zip(carry, (r, r + middle)):
-            value = plan[SEGMENT + at_r // DEVICES, lax.rem(at_r, DEVICES)]
-            slot, b = value // CHIPS, lax.rem(value, CHIPS)
-            total = jnp.where(b == previous, total, 0.0) + results[slot]
-            running[at_r] = total
+        for h, (total, previous) in enumerate(carry):
+            value = plan[SEGMENT + h, r]
+            b = value & (CHIPS - 1)
+            total = jnp.where(b == previous, total, 0.0) + results[value >> 6]
+            running[h * middle + r] = total
             new.append((total, b))
         return tuple(new)
 
     none = (jnp.zeros(running.shape[1:], jnp.float32), jnp.int32(-1))
-    lax.fori_loop(0, middle, add, (none, none), unroll=4)
+    lax.fori_loop(0, middle, add, (none, none), unroll=8)
 
     def finished(b):
         upto = plan[UPTO, b]

time: 86.7 us -> 97 us (1.12); the launches traced: 86.6 us -> 95.6 us
  Pallas kernels: 83.8 us -> 92.9 us
    pallas_call x1, Pallas kernels: 81.8 us -> 90.9 us  [exchange(): pl.pallas_call(functools.partial(exchange_kernel, shared), out_shape=(jax...]
where the time goes in v5:
time: 97 us; the launch traced here: 95.6 us
  Pallas kernels  92.9 us (96%)
  local copies, waits for them, and re-layouts  1.43 us (1%)
  between operations  1.3 us (1%)
    pallas_call x1, Pallas kernels, exchange(): pl.pallas_call(functools.partial(exchange_kernel, shared), out_shape=(jax...  90.9 us
    pallas_call x1, Pallas kernels, per_device(): pl.pallas_call(plan_kernel, out_shape=(jax.ShapeDtypeStruct((ROWS, DEVICE...  2 us

profile of v5, /device:TPU:1, one launch (start us, length us, event | category | flops | bytes accessed | tf_op | source)
XLA Modules:
  0.0 95.6 jit_solution(7176346317442305353)
XLA Ops:
  0.6 2.0 %plan.1 = (s32[16,128]{1,0:T(8,128)S(1)}, s32[1]{0:T(128)}) custom-call(s32[256,128]{1,0:T(8,128)} %bitcast.13, s32[256,128]{1,0:T(8,128)} %bitcast.14, s32[2,128]{1,0:T(2,128)} %bitcast.18), custom_call_target="tpu_custom_call" | custom-call | tf_op jit(solution)/shard_map/plan/pallas_call | solution.py:368
  3.3 90.9 %conditional.1 = ((bf16[30,64,128]{2,1,0:T(8,128)(2,1)S(1)}, bf16[2,30,8,128]{3,2,1,0:T(8,128)(2,1)S(1)})) conditional(s32[]{:T(128)} %bitcast.3, (s32[16,128]{1,0:T(8,128)S(1)}, s32[2,8]{1,0:T(2,128)}, bf16[30,128,256]{2,1,0:T(8,128)(2,1)}, bf16[256,256,128]{2,1,0:T(8,128)(2,1)}, f32[64,128]{1,0:T(8,128)}) %tuple.24, (s32[16,128]{1,0:T(8,128)S(1)}, ...), branch_computations={%region_0.0_spmd, %region_1.0_spmd} | conditional | bytes 8 | solution.py:375
  3.3 90.9 %remap_direct.1 = (bf16[30,64,128]{2,1,0:T(8,128)(2,1)S(1)}, bf16[2,30,8,128]{3,2,1,0:T(8,128)(2,1)S(1)}) custom-call(s32[16,128]{1,0:T(8,128)S(1)} %get-tuple-element.20.plan, s32[2,8]{1,0:T(2,128)} %get-tuple-element.21.halo_idx, bf16[30,128,256]{2,1,0:T(8,128)(2,1)} %get-tuple-element.22.atm_by_field, bf16[256,256,128]{2,1,0:T(8,128)(2,1)} %get-tuple-element.23.weights, ...), custom_call_target="tpu_custom_call" | custom-call | tf_op jit(solution)/shard_map/cond/branch_0_fun/remap_direct/pallas_call | solution.py:326
  94.2 0.8 copy.15
  95.0 0.6 copy.16

commit v6 on v5

--- a/solution.py
+++ b/solution.py
@@ -101,8 +101,8 @@
 
 
 def exchange_kernel(
-    shared, plan, halo_idx, atm_by_field, weights, frac, out_hbm, halo_hbm,
-    atm, out_far, out_same, in_far, in_same, lent, borrowed, near, near_out, w_vmem, results, running, fields, rim,
+    shared, plan, halo_idx, atm_hbm, weights, frac_hbm, out_hbm, halo_hbm,
+    atm_by_field, frac, input_sem, atm, out_far, out_same, in_far, in_same, lent, borrowed, near, near_out, w_vmem, results, running, fields, rim,
     send_sem, far_sem, same_sem, lend_sem, near_sem, w_sem, rim_send, rim_recv, out_sem,
 ):
     gx, gy = lax.axis_index("gx"), lax.axis_index("gy")
@@ -124,6 +124,10 @@
     def index(chip, core):
         return chip[0] * 32 + core * 16 + chip[1]
 
+    atm_copy = pltpu.make_async_copy(atm_hbm, atm_by_field, input_sem.at[0])
+    atm_copy.start()
+    frac_copy = pltpu.make_async_copy(frac_hbm, frac, input_sem.at[1])
+    frac_copy.start()
     partner = (x * 2 + other, gy)
     barrier = pltpu.get_barrier_semaphore()
     pl.semaphore_signal(barrier, inc=1, device_id=partner, device_id_type=MESH)
@@ -131,11 +135,12 @@
     @pl.loop(0, STEPS)
     def _(i):
         for core in (0, 1):
-            pl.semaphore_signal(barrier, inc=1, device_id=at(chip_at(i, 1), core), device_id_type=MESH)
+            pl.semaphore_signal(barrier, inc=1, device_id=at(chip_at(i, 1 - 2 * c), core), device_id_type=MESH)
 
     w_copy = pltpu.make_async_copy(weights, w_vmem, w_sem)
     w_copy.start()
 
+    atm_copy.wait()
     rows = 16
 
     @pl.loop(0, atm.shape[0] // rows)
@@ -181,7 +186,7 @@
     )
 
     def send_far(i):
-        chip = chip_at(i, 1)
+        chip = chip_at(i, 1 - 2 * c)
         d = index(chip, other)
         out_far[i] = pack([block(d, k) for k in range(far_cap)])
         pltpu.make_async_remote_copy(
@@ -190,7 +195,7 @@
         ).start()
 
     def send_same(i):
-        chip = chip_at(i, 1)
+        chip = chip_at(i, 1 - 2 * c)
         d = index(chip, c)
         blocks = [block(d, k) for k in range(CAP)]
         if shared:
@@ -215,10 +220,10 @@
         pltpu.make_async_copy(in_same.at[i], in_same.at[i], same_sem.at[i]).wait()
 
     def take_far(i):
-        multiply(index(chip_at(i, -1), other), [unpack(in_far, i, k) for k in range(far_cap)])
+        multiply(index(chip_at(i, 1 - 2 * c), other), [unpack(in_far, i, k) for k in range(far_cap)])
 
     def take_same(i):
-        multiply(index(chip_at(i, -1), c), [unpack(in_same, i, k) for k in range(CAP)])
+        multiply(index(chip_at(i, 2 * c - 1), c), [unpack(in_same, i, k) for k in range(CAP)])
 
     @pl.loop(0, STEPS)
     def _(i):
@@ -232,6 +237,7 @@
     def _(i):
         send_same(i)
 
+    frac_copy.wait()
     w_copy.wait()
     multiply(myself, [near[CAP + k] for k in range(CAP)])
     near_copy.wait()
@@ -277,11 +283,10 @@
         return jnp.swapaxes(jnp.stack(blocks), 0, 1).astype(jnp.bfloat16)
 
     rim_n = rim.shape[2]
-    for side in (0, 1):
-        rim[side] = by_field([finished(halo_idx[side, j]) for j in range(rim_n)])
     up, down = lax.rem(myself + 1, DEVICES), lax.rem(myself + DEVICES - 1, DEVICES)
     rim_copies = []
     for side, there in ((1, up), (0, down)):
+        rim[side] = by_field([finished(halo_idx[side, j]) for j in range(rim_n)])
         copy = pltpu.make_async_remote_copy(
             src_ref=rim.at[side],
             dst_ref=halo_hbm.at[1 - side],
@@ -312,7 +317,6 @@
     fields_n, blocks_n = atm_by_field.shape[:2]
     ocean_n, rim_n = frac.shape[0], halo_idx.shape[1]
     smem = pl.BlockSpec(memory_space=pltpu.SMEM)
-    vmem = pl.BlockSpec(memory_space=pltpu.VMEM)
     hbm = pl.BlockSpec(memory_space=pl.ANY)
     far_cap = CAP - 1 if shared else CAP
     lent_n = CHIPS if shared else 1
@@ -329,9 +333,12 @@
             jax.ShapeDtypeStruct((fields_n, ocean_n, cells), jnp.bfloat16),
             jax.ShapeDtypeStruct((2, fields_n, rim_n, cells), jnp.bfloat16),
         ),
-        in_specs=[smem, smem, vmem, hbm, vmem],
+        in_specs=[smem, smem, hbm, hbm, hbm],
         out_specs=(hbm, hbm),
         scratch_shapes=[
+            pltpu.VMEM(atm_by_field.shape, jnp.bfloat16),
+            pltpu.VMEM(frac.shape, jnp.float32),
+            pltpu.SemaphoreType.DMA((2,)),
             blocks(blocks_n),
             messages(STEPS, far_cap),
             messages(STEPS, CAP),

time: 97 us -> 83.1 us (0.86); the launches traced: 95.6 us -> 82.9 us
  Pallas kernels: 92.9 us -> 80.2 us
    pallas_call x1, Pallas kernels: 90.9 us -> 78.2 us  [exchange(): pl.pallas_call(functools.partial(exchange_kernel, shared), out_shape=(jax...]
where the time goes in v6:
time: 83.1 us; the launch traced here: 82.9 us
  Pallas kernels  80.2 us (97%)
  local copies, waits for them, and re-layouts  1.43 us (2%)
  between operations  1.3 us (2%)
    pallas_call x1, Pallas kernels, exchange(): pl.pallas_call(functools.partial(exchange_kernel, shared), out_shape=(jax...  78.2 us
    pallas_call x1, Pallas kernels, per_device(): pl.pallas_call(plan_kernel, out_shape=(jax.ShapeDtypeStruct((ROWS, DEVICE...  2 us

profile of v6, /device:TPU:1, one launch (start us, length us, event | category | flops | bytes accessed | tf_op | source)
XLA Modules:
  0.0 82.9 jit_solution(13664551632473852725)
XLA Ops:
  0.6 2.0 %plan.1 = (s32[16,128]{1,0:T(8,128)S(1)}, s32[1]{0:T(128)}) custom-call(s32[256,128]{1,0:T(8,128)} %bitcast.13, s32[256,128]{1,0:T(8,128)} %bitcast.14, s32[2,128]{1,0:T(2,128)} %bitcast.18), custom_call_target="tpu_custom_call" | custom-call | tf_op jit(solution)/shard_map/plan/pallas_call | solution.py:375
  3.3 78.2 %conditional.1 = ((bf16[30,64,128]{2,1,0:T(8,128)(2,1)S(1)}, bf16[2,30,8,128]{3,2,1,0:T(8,128)(2,1)S(1)})) conditional(s32[]{:T(128)} %bitcast.3, (s32[16,128]{1,0:T(8,128)S(1)}, s32[2,8]{1,0:T(2,128)}, bf16[30,128,256]{2,1,0:T(8,128)(2,1)}, bf16[256,256,128]{2,1,0:T(8,128)(2,1)}, f32[64,128]{1,0:T(8,128)}) %tuple.24, (s32[16,128]{1,0:T(8,128)S(1)}, ...), branch_computations={%region_0.0_spmd, %region_1.0_spmd} | conditional | bytes 8 | solution.py:382
  3.3 78.2 %remap_shared.1 = (bf16[30,64,128]{2,1,0:T(8,128)(2,1)S(1)}, bf16[2,30,8,128]{3,2,1,0:T(8,128)(2,1)S(1)}) custom-call(s32[16,128]{1,0:T(8,128)S(1)} %get-tuple-element.25.plan, s32[2,8]{1,0:T(2,128)} %get-tuple-element.26.halo_idx, bf16[30,128,256]{2,1,0:T(8,128)(2,1)} %get-tuple-element.27.atm_hbm, bf16[256,256,128]{2,1,0:T(8,128)(2,1)} %get-tuple-element.28.weights, ...), custom_call_target="tpu_custom_call" | custom-call | tf_op jit(solution)/shard_map/cond/branch_1_fun/remap_shared/pallas_call | solution.py:330
  81.5 0.8 copy.15
  82.3 0.6 copy.16

commit v7 on v6

--- a/solution.py
+++ b/solution.py
@@ -130,12 +130,17 @@
     frac_copy.start()
     partner = (x * 2 + other, gy)
     barrier = pltpu.get_barrier_semaphore()
-    pl.semaphore_signal(barrier, inc=1, device_id=partner, device_id_type=MESH)
-
-    @pl.loop(0, STEPS)
+    def greet(ahead):
+        there = lax.rem(myself + ahead, DEVICES)
+        device = (there // 16, lax.rem(there, 16))
+        pl.semaphore_signal(barrier, inc=1, device_id=device, device_id_type=MESH)
+
+    greet(DEVICES - 1)
+
+    @pl.loop(0, (DEVICES - 2) // 7)
     def _(i):
-        for core in (0, 1):
-            pl.semaphore_signal(barrier, inc=1, device_id=at(chip_at(i, 1 - 2 * c), core), device_id_type=MESH)
+        for j in range(7):
+            greet(i * 7 + j + 1)
 
     w_copy = pltpu.make_async_copy(weights, w_vmem, w_sem)
     w_copy.start()

time: 83.1 us -> 82.5 us (level)
  no operation moved by 1% of the time
where the time goes in v7:
time: 82.5 us; the launch traced here: 82.3 us
  Pallas kernels  79.6 us (96%)
  local copies, waits for them, and re-layouts  1.43 us (2%)
  between operations  1.3 us (2%)
    pallas_call x1, Pallas kernels, exchange(): pl.pallas_call(functools.partial(exchange_kernel, shared), out_shape=(jax...  77.6 us
    pallas_call x1, Pallas kernels, per_device(): pl.pallas_call(plan_kernel, out_shape=(jax.ShapeDtypeStruct((ROWS, DEVICE...  2 us

profile of v7, /device:TPU:1, one launch (start us, length us, event | category | flops | bytes accessed | tf_op | source)
XLA Modules:
  0.0 82.3 jit_solution(3889346701510111168)
XLA Ops:
  0.6 2.0 %plan.1 = (s32[16,128]{1,0:T(8,128)S(1)}, s32[1]{0:T(128)}) custom-call(s32[256,128]{1,0:T(8,128)} %bitcast.13, s32[256,128]{1,0:T(8,128)} %bitcast.14, s32[2,128]{1,0:T(2,128)} %bitcast.18), custom_call_target="tpu_custom_call" | custom-call | tf_op jit(solution)/shard_map/plan/pallas_call | solution.py:380
  3.3 77.6 %conditional.1 = ((bf16[30,64,128]{2,1,0:T(8,128)(2,1)S(1)}, bf16[2,30,8,128]{3,2,1,0:T(8,128)(2,1)S(1)})) conditional(s32[]{:T(128)} %bitcast.3, (s32[16,128]{1,0:T(8,128)S(1)}, s32[2,8]{1,0:T(2,128)}, bf16[30,128,256]{2,1,0:T(8,128)(2,1)}, bf16[256,256,128]{2,1,0:T(8,128)(2,1)}, f32[64,128]{1,0:T(8,128)}) %tuple.24, (s32[16,128]{1,0:T(8,128)S(1)}, ...), branch_computations={%region_0.0_spmd, %region_1.0_spmd} | conditional | bytes 8 | solution.py:387
  3.3 77.6 %remap_shared.1 = (bf16[30,64,128]{2,1,0:T(8,128)(2,1)S(1)}, bf16[2,30,8,128]{3,2,1,0:T(8,128)(2,1)S(1)}) custom-call(s32[16,128]{1,0:T(8,128)S(1)} %get-tuple-element.25.plan, s32[2,8]{1,0:T(2,128)} %get-tuple-element.26.halo_idx, bf16[30,128,256]{2,1,0:T(8,128)(2,1)} %get-tuple-element.27.atm_hbm, bf16[256,256,128]{2,1,0:T(8,128)(2,1)} %get-tuple-element.28.weights, ...), custom_call_target="tpu_custom_call" | custom-call | tf_op jit(solution)/shard_map/cond/branch_1_fun/remap_shared/pallas_call | solution.py:335
  80.9 0.8 copy.15
  81.7 0.6 copy.16
